TPU v7x, 32 devices: a whole 2x2x4 slice. The times are simulated.
32 devices in a mesh: seq: 4 (over y, x), tensor: 8 (over z, core).
Axes of the slice: x: 2, y: 2, z: 4, core: 2. Of those that a mesh axis runs over, the one named last changes fastest.
Arguments:
- tokens: bfloat16 [1024, 4096], P(('seq', 'tensor')), may hold values from -6 to 6
- w_gate: bfloat16 [4096, 8192], P('seq', 'tensor'), may hold values from -0.09375 to 0.09375
- w_xin: bfloat16 [4096, 8192], P('seq', 'tensor'), may hold values from -0.09375 to 0.09375
- w_bc: bfloat16 [4096, 2048], P('seq', 'tensor'), may hold values from -0.09375 to 0.09375
- w_dt: bfloat16 [4096, 128], P('seq', 'tensor'), may hold values from -0.09375 to 0.09375
- conv_x: float32 [4, 8192], P(None, 'tensor'), may hold values from -3 to 3
- conv_x_bias: float32 [8192], P('tensor'), may hold values from -3 to 3
- conv_bc: float32 [4, 2048], P(None, 'tensor'), may hold values from -3 to 3
- conv_bc_bias: float32 [2048], P('tensor'), may hold values from -3 to 3
- dt_bias: float32 [128], P('tensor'), may hold values from -1 to 1
- decay_rate: float32 [128], P('tensor'), may hold values from 0.000390625 to 0.08, as said below
- d_skip: float32 [128], P('tensor'), may hold values from 0.5 to 1.5
- norm_gain: float32 [8192], P('tensor'), may hold values from 0.25 to 1.75
- w_out: bfloat16 [8192, 4096], P('tensor', 'seq'), may hold values from -0.0625 to 0.0625
- lengths: int32 [8], replicated, may hold values from 1 to 512, 1024 in all
Outputs:
- mixed: bfloat16 [1024, 4096], P(('seq', 'tensor'))
Inputs may be any that keep to these rules, and one draw needn't show every extreme that they name: lengths of 8 prompts that fill the pack of 1024 tokens exactly; the longest is exactly 512. `decay_rate`: positive rates.
All inputs are finite; a program needn't handle non-finite values.
Results may differ from a plain program's by a relative error of at most 0.03.
Values may be sent and summed in bfloat16 or wider, within the bound.
A program may use at most 64 MiB of HBM per device.

v0:
```python
import jax
import jax.numpy as jnp
import numpy as np
from jax import lax
from jax.experimental import pallas as pl
from jax.experimental.pallas import tpu as pltpu
from jax.sharding import PartitionSpec as P

HDIM = 64
GROUPS = 8
STATE = 128
CONV = 4
STRETCH = 256
INNER = 8192


HIGH = lax.Precision.HIGHEST


def from_behind(x, axis, by):
    count = lax.axis_size(axis)
    pairs = [(i, i + by) for i in range(count) if 0 <= i + by < count]
    return lax.ppermute(x, axis, pairs)


def carried_in(x, axis, combine, identity):
    count, here = (lax.axis_size(axis), lax.axis_index(axis))
    everything = jax.tree.map(
        lambda part, kind: lax.all_gather(part.astype(kind), axis), x, (jnp.bfloat16, jnp.bfloat16)
    )
    start = jax.tree.map(
        lambda part, zero: jnp.broadcast_to(jnp.asarray(zero, part.dtype), part.shape), x, identity
    )

    def hop(k, before):
        reached = k < here
        new = combine(
            before, jax.tree.map(lambda part, own: part[k].astype(own.dtype), everything, x)
        )
        return jax.tree.map(lambda a, b: jnp.where(reached, a, b), new, before)

    return lax.fori_loop(0, count, hop, start)


def doc_ids(lengths, positions):
    starts = jnp.cumsum(lengths) - lengths
    counted = jnp.sum((starts[None, :] <= positions[:, None]).astype(jnp.int32), axis=1)
    return counted - 1


def causal_conv(values, edge, weights, bias, docs, edge_docs):
    count = values.shape[0]
    extended = jnp.concatenate([edge, values], axis=0).astype(jnp.float32)
    all_docs = jnp.concatenate([edge_docs, docs])
    summed = jnp.zeros(values.shape, jnp.float32) + bias[None, :]
    for offset in range(weights.shape[0]):
        same = (all_docs[offset : offset + count] == docs).astype(jnp.float32)
        summed = (
            summed + weights[offset][None, :] * extended[offset : offset + count] * same[:, None]
        )
    return lax.optimization_barrier(jax.nn.silu(summed).astype(jnp.bfloat16))


def ssd_blocks(xvals, dtv, rate, bmat, cmat, docs, prev_doc, head_group, block):
    count, heads, hdim = xvals.shape
    nstate = bmat.shape[2]
    blocks = count // block
    logs = -dtv * rate[None, :]

    def split(array):
        return array.reshape((blocks, block) + array.shape[1:])

    lower = jnp.tril(jnp.ones((block, block), bool))

    def step(carry, pieces):
        state, last_doc = carry
        xblk, dblk, lblk, bblk, cblk, docblk = pieces
        cum = jnp.cumsum(lblk, axis=0)
        same = (docblk[:, None] == docblk[None, :]) & lower
        diff = cum.T[:, :, None] - cum.T[:, None, :]
        decay = jnp.exp(jnp.where(same[None], diff, -jnp.inf))
        scores = jnp.einsum("ign,jgn->gij", cblk, bblk, precision=HIGH)
        mixing = scores[head_group] * decay * dblk.T[:, None, :]
        inner = jnp.einsum("hij,jhp->ihp", mixing, xblk, precision=HIGH)
        open_in = (docblk == last_doc).astype(jnp.float32)
        carry_in = jnp.exp(cum) * open_in[:, None]
        chead = cblk[:, head_group, :]
        outer = jnp.einsum("ihn,hpn->ihp", chead, state, precision=HIGH) * carry_in[:, :, None]
        end_doc = docblk[-1]
        tail = (
            jnp.exp(cum[-1][None, :] - cum)
            * (docblk == end_doc).astype(jnp.float32)[:, None]
            * dblk
        )
        bhead = bblk[:, head_group, :]
        fresh = jnp.einsum("jh,jhp,jhn->hpn", tail, xblk, bhead, precision=HIGH)
        state = carry_in[-1][:, None, None] * state + fresh
        return ((state, end_doc), inner + outer)

    init = (jnp.zeros((heads, hdim, nstate), jnp.float32), prev_doc)
    (state, end_doc), outs = lax.scan(
        step, init, (split(xvals), split(dtv), split(logs), split(bmat), split(cmat), split(docs))
    )
    return (outs.reshape(count, heads, hdim), state)


def shards_wide(
    tokens,
    w_gate,
    w_xin,
    w_bc,
    w_dt,
    conv_x,
    conv_x_bias,
    conv_bc,
    conv_bc_bias,
    dt_bias,
    decay_rate,
    d_skip,
    norm_gain,
    w_out,
    lengths,
):
    tensor_count = lax.axis_size("tensor")
    seq_index = lax.axis_index("seq")
    tensor_index = lax.axis_index("tensor")
    span_rows = lax.all_gather(tokens, "tensor", axis=0, tiled=True)
    span_len = span_rows.shape[0]
    pieces = (
        lax.all_gather(w_gate, "seq", axis=0, tiled=True),
        lax.all_gather(w_xin, "seq", axis=0, tiled=True),
        lax.all_gather(w_bc, "seq", axis=0, tiled=True),
        lax.all_gather(w_dt, "seq", axis=0, tiled=True),
    )
    gate_acc, xin_acc, bc_acc, dt_acc = tuple(
        (
            jnp.dot(span_rows, weight_piece, preferred_element_type=jnp.float32)
            for weight_piece in pieces
        )
    )
    gate = gate_acc.astype(jnp.bfloat16)
    xin = xin_acc.astype(jnp.bfloat16)
    bcin = bc_acc.astype(jnp.bfloat16)
    dtin = dt_acc.astype(jnp.bfloat16)
    gate, xin, bcin, dtin = lax.optimization_barrier((gate, xin, bcin, dtin))
    positions = seq_index * span_len + jnp.arange(span_len, dtype=jnp.int32)
    docs = doc_ids(lengths, positions)
    edge_docs = doc_ids(lengths, seq_index * span_len + jnp.arange(-(CONV - 1), 0, dtype=jnp.int32))
    prev_span_doc = doc_ids(lengths, positions[:1] - 1)[0]
    edge_x, edge_bc = from_behind(
        (xin[span_len - (CONV - 1) :], bcin[span_len - (CONV - 1) :]), "seq", 1
    )
    x_conv = causal_conv(xin, edge_x, conv_x, conv_x_bias, docs, edge_docs)
    bc_conv = causal_conv(bcin, edge_bc, conv_bc, conv_bc_bias, docs, edge_docs)
    group_span = tensor_count // GROUPS
    my_group = tensor_index // group_span
    every_group = lax.all_gather(bc_conv, "tensor", axis=1, tiled=True)
    arranged = every_group.reshape(span_len, 2 * STATE, GROUPS)
    group_cols = lax.dynamic_slice_in_dim(arranged, my_group, 1, 2).reshape(span_len, 2 * STATE)
    head_dev = w_dt.shape[1]
    head_group = np.zeros(head_dev, dtype=np.int32)
    both = group_cols.astype(jnp.float32)
    bmat = both[:, None, :STATE]
    cmat = both[:, None, STATE:]
    xvals = x_conv.astype(jnp.float32).reshape(span_len, head_dev, HDIM)
    dtv = jax.nn.softplus(dtin.astype(jnp.float32) + dt_bias[None, :])
    block = min(STRETCH, span_len)
    y_local, end_state = ssd_blocks(
        xvals, dtv, decay_rate, bmat, cmat, docs, prev_span_doc, head_group, block
    )
    cum_span = jnp.cumsum(-dtv * decay_rate[None, :], axis=0)
    open_span = (docs == prev_span_doc).astype(jnp.float32)
    span_decay = jnp.exp(cum_span[-1]) * open_span[-1]

    def combine(earlier, later):
        return (earlier[0] * later[0], later[0][:, None, None] * earlier[1] + later[1])

    entering = carried_in(
        (span_decay, end_state),
        "seq",
        combine,
        (jnp.ones_like(span_decay), jnp.zeros_like(end_state)),
    )[1]
    carried = jnp.exp(cum_span) * open_span[:, None]
    y_enter = (
        jnp.einsum("ihn,hpn->ihp", cmat[:, head_group, :], entering, precision=HIGH)
        * carried[:, :, None]
    )
    yvals = (y_local + y_enter + d_skip[None, :, None] * xvals).reshape(span_len, head_dev * HDIM)
    gated = yvals * jax.nn.silu(gate.astype(jnp.float32))
    local_sq = jnp.sum(gated * gated, axis=1)
    group_mark = (jnp.arange(GROUPS) == my_group).astype(jnp.float32)
    every_sum = lax.psum(local_sq[:, None] * group_mark[None, :], "tensor")
    group_mean = jnp.sum(every_sum * group_mark[None, :], axis=1) / (INNER // GROUPS)
    normed = (gated * lax.rsqrt(group_mean + 1e-05)[:, None] * norm_gain[None, :]).astype(
        jnp.bfloat16
    )
    w_full = lax.all_gather(w_out, "seq", axis=1, tiled=True)
    return lax.psum_scatter(
        jnp.dot(normed, w_full, preferred_element_type=jnp.float32).astype(jnp.bfloat16),
        "tensor",
        scatter_dimension=0,
        tiled=True,
    )


def enter(peers):
    barrier = pltpu.get_barrier_semaphore()
    for peer in peers:
        pl.semaphore_signal(barrier, inc=1, device_id=peer, device_id_type=pl.DeviceIdType.MESH)
    pl.semaphore_wait(barrier, len(peers))


def remote(src, dst, send, recv, peer):
    return pltpu.make_async_remote_copy(
        src_ref=src,
        dst_ref=dst,
        send_sem=send,
        recv_sem=recv,
        device_id=peer,
        device_id_type=pl.DeviceIdType.MESH,
    )


def places():
    s, t = lax.axis_index("seq"), lax.axis_index("tensor")
    seqs, chips = lax.axis_size("seq"), lax.axis_size("tensor") // 2
    z, c = t // 2, t % 2

    def along(ds, dz):
        return lax.rem(s + ds, seqs), lax.rem(z + dz, chips)

    return s, z, c, seqs, chips, along


def out_kernel(
    g_ref, gain_ref, w_ref, out_ref, held, normed, part, sib, pair, got,
    g_send, g_recv, p_send, p_recv, o_send, o_recv,
):
    s, z, c, seqs, chips, along = places()
    span = g_ref.shape[0] // seqs
    width = g_ref.shape[1]
    own = out_ref.shape[0]
    cols = w_ref.shape[1]
    sibling = (s, 2 * z + 1 - c)
    offsets = [(ds, dz) for ds in range(seqs) for dz in range(chips) if ds or dz]
    enter([(along(ds, dz)[0], 2 * along(ds, dz)[1] + c) for ds, dz in offsets] + [sibling])
    order = list(range(1, seqs)) + [0]
    gathers = {}
    for k in order:
        for ds in range(1, seqs):
            rows = pl.ds(pl.multiple_of(lax.rem(s + ds + k, seqs) * span, span), span)
            gathers[k, ds] = remote(
                g_ref.at[rows],
                held.at[ds, rows],
                g_send.at[k, ds],
                g_recv.at[k, ds],
                (along(ds, 0)[0], 2 * z + c),
            )
            gathers[k, ds].start()
    pairs, sends = {}, []

    def finish(k):
        q = lax.rem(s + k, seqs)
        pairs[k].wait_recv()
        for dz in range(chips):
            there = along(0, dz)[1]
            both = part[q, there, c].astype(jnp.float32) + sib[q, there].astype(jnp.float32)
            if k == 0 and dz == 0:
                got[0, 0] = both.astype(jnp.bfloat16)
            else:
                pair[k, dz] = both.astype(jnp.bfloat16)
                sends.append(
                    remote(
                        pair.at[k, dz],
                        got.at[k, dz],
                        o_send.at[k, dz],
                        o_recv.at[k, dz],
                        (q, 2 * there + c),
                    )
                )
                sends[-1].start()

    for step, k in enumerate(order):
        q = lax.rem(s + k, seqs)
        rows = pl.ds(pl.multiple_of(q * span, span), span)
        for ds in range(1, seqs):
            gathers[k, ds].wait_recv()
        blocks = [g_ref[rows, :].astype(jnp.float32)] + [
            held[ds, rows, :].astype(jnp.float32) for ds in range(1, seqs)
        ]
        squares = blocks[0] * blocks[0]
        for b in blocks[1:]:
            squares = squares + b * b
        scale = lax.rsqrt(jnp.sum(squares, axis=1, keepdims=True) / (width * seqs) + 1e-05)
        froms = [pl.multiple_of(lax.rem(s + seqs - ds, seqs) * width, width) for ds in range(seqs)]
        for ds in range(seqs):
            normed[ds] = (blocks[ds] * scale * gain_ref[:, pl.ds(froms[ds], width)]).astype(
                jnp.bfloat16
            )
        tile = 256

        def column(n, _):
            here = pl.ds(pl.multiple_of(n * tile, tile), tile)
            acc = jnp.zeros((span, tile), jnp.float32)
            for ds in range(seqs):
                acc = acc + jnp.dot(
                    normed[ds],
                    w_ref[pl.ds(froms[ds], width), here],
                    preferred_element_type=jnp.float32,
                )
            part[q, :, :, :, here] = acc.astype(jnp.bfloat16).reshape(chips, 2, own, tile)
            return 0

        lax.fori_loop(0, cols // tile, column, 0)
        pairs[k] = remote(
            part.at[q, :, 1 - c], sib.at[q], p_send.at[k], p_recv.at[k], sibling
        )
        pairs[k].start()
        if step:
            finish(order[step - 1])
    finish(order[-1])
    for copy in sends:
        copy.wait_recv()
    for ds in range(seqs):
        total = got[ds, 0].astype(jnp.float32)
        for dz in range(1, chips):
            total = total + got[ds, dz].astype(jnp.float32)
        begin = pl.multiple_of(lax.rem(s + seqs - ds, seqs) * cols, cols)
        out_ref[:, pl.ds(begin, cols)] = total.astype(jnp.bfloat16)
    for copy in list(gathers.values()) + list(pairs.values()) + sends:
        copy.wait_send()


def project_out(gated, gain, w_out, own, seqs, chips):
    total, width = gated.shape
    cols = w_out.shape[1]
    dma = pltpu.SemaphoreType.DMA
    vmem = pl.BlockSpec(memory_space=pltpu.VMEM)
    return pl.pallas_call(
        out_kernel,
        out_shape=jax.ShapeDtypeStruct((own, cols * seqs), jnp.bfloat16),
        in_specs=[vmem] * 3,
        out_specs=vmem,
        scratch_shapes=[
            pltpu.VMEM((seqs, total, width), jnp.bfloat16),
            pltpu.VMEM((seqs, total // seqs, width), jnp.bfloat16),
            pltpu.VMEM((seqs, chips, 2, own, cols), jnp.bfloat16),
            pltpu.VMEM((seqs, chips, own, cols), jnp.bfloat16),
            pltpu.VMEM((seqs, chips, own, cols), jnp.bfloat16),
            pltpu.VMEM((seqs, chips, own, cols), jnp.bfloat16),
            dma((seqs, seqs)),
            dma((seqs, seqs)),
            dma((seqs,)),
            dma((seqs,)),
            dma((seqs, chips)),
            dma((seqs, chips)),
        ],
        compiler_params=pltpu.CompilerParams(
            collective_id=1, has_side_effects=True, vmem_limit_bytes=40 * 2**20
        ),
    )(gated, gain[None, :], w_out)


def in_kernel(
    tok_ref, wg_ref, wx_ref, ws_ref, gate_ref, xin_ref, small_ref,
    tok, mine, mine_s, sent, sent_s, got, got_s,
    t_send, t_recv, f_send, f_recv, p_send, p_recv, q_send, q_recv,
):
    s, z, c, seqs, chips, along = places()
    own = tok_ref.shape[0]
    depth = wg_ref.shape[0]
    width = wg_ref.shape[1] // seqs
    span = own * chips * 2
    sibling = (s, 2 * z + 1 - c)
    offsets = [(ds, dz) for ds in range(seqs) for dz in range(chips) if ds or dz]
    enter([(along(ds, dz)[0], 2 * along(ds, dz)[1] + c) for ds, dz in offsets] + [sibling])
    spread = {}
    for ds, dz in offsets:
        to, there = along(ds, dz)
        spread[ds, dz] = remote(
            tok_ref.at[:, pl.ds(pl.multiple_of(to * depth, depth), depth)],
            tok.at[ds, z, c],
            t_send.at[ds, dz],
            t_recv.at[ds, dz],
            (to, 2 * there + c),
        )
        spread[ds, dz].start()
    tok[0, z, c] = tok_ref[:, pl.ds(pl.multiple_of(s * depth, depth), depth)]
    forwards, sums = [], []

    def forward(k):
        for ds, dz in offsets:
            if ds == k:
                spread[ds, dz].wait_recv()
        forwards.append(
            remote(tok.at[k, :, c], tok.at[k, :, c], f_send.at[k], f_recv.at[k], sibling)
        )
        forwards[k].start()

    forward(0)
    for k in range(seqs):
        forwards[k].wait_recv()
        if k + 1 < seqs:
            forward(k + 1)
        q = lax.rem(s + seqs - k, seqs)
        for ds in list(range(1, seqs)) + [0]:
            to = along(ds, 0)[0]
            cols = pl.ds(pl.multiple_of(to * width, width), width)
            rows = tok[k].reshape(span, depth)
            gate = jnp.dot(rows, wg_ref[:, cols], preferred_element_type=jnp.float32)
            xin = jnp.dot(rows, wx_ref[:, cols], preferred_element_type=jnp.float32)
            small = lax.dot_general(
                ws_ref[to], rows, (((1,), (1,)), ((), ())), preferred_element_type=jnp.float32
            )
            if ds == 0:
                mine[q, :, :width] = gate
                mine[q, :, width:] = xin
                mine_s[q] = small
                continue
            sent[ds, k, :, :width] = gate.astype(jnp.bfloat16)
            sent[ds, k, :, width:] = xin.astype(jnp.bfloat16)
            sent_s[ds, k] = small.astype(jnp.bfloat16)
            peer = (to, 2 * z + c)
            for copy in (
                remote(sent.at[ds, k], got.at[ds, q], p_send.at[ds, k], p_recv.at[ds, k], peer),
                remote(
                    sent_s.at[ds, k], got_s.at[ds, q], q_send.at[ds, k], q_recv.at[ds, k], peer
                ),
            ):
                copy.start()
                sums.append(copy)
    for copy in sums:
        copy.wait_recv()

    def add(q, _):
        rows = pl.ds(pl.multiple_of(q * span, span), span)
        total, small = mine[q], mine_s[q]
        for ds in range(1, seqs):
            total = total + got[ds, q].astype(jnp.float32)
            small = small + got_s[ds, q].astype(jnp.float32)
        gate_ref[rows, :] = total[:, :width].astype(jnp.bfloat16)
        xin_ref[rows, :] = total[:, width:].astype(jnp.bfloat16)
        small_ref[:, rows] = small.astype(jnp.bfloat16)
        return 0

    lax.fori_loop(0, seqs, add, 0)
    for copy in list(spread.values()) + forwards + sums:
        copy.wait_send()


def project_in(tokens, w_gate, w_xin, w_small, seqs, chips):
    own = tokens.shape[0]
    depth = w_gate.shape[0]
    width = w_gate.shape[1] // seqs
    span = own * chips * 2
    few = w_small.shape[1]
    dma = pltpu.SemaphoreType.DMA
    vmem = pl.BlockSpec(memory_space=pltpu.VMEM)
    return pl.pallas_call(
        in_kernel,
        out_shape=(
            jax.ShapeDtypeStruct((span * seqs, width), jnp.bfloat16),
            jax.ShapeDtypeStruct((span * seqs, width), jnp.bfloat16),
            jax.ShapeDtypeStruct((few, span * seqs), jnp.bfloat16),
        ),
        in_specs=[vmem] * 4,
        out_specs=(vmem,) * 3,
        scratch_shapes=[
            pltpu.VMEM((seqs, chips, 2, own, depth), jnp.bfloat16),
            pltpu.VMEM((seqs, span, 2 * width), jnp.float32),
            pltpu.VMEM((seqs, few, span), jnp.float32),
            pltpu.VMEM((seqs, seqs, span, 2 * width), jnp.bfloat16),
            pltpu.VMEM((seqs, seqs, few, span), jnp.bfloat16),
            pltpu.VMEM((seqs, seqs, span, 2 * width), jnp.bfloat16),
            pltpu.VMEM((seqs, seqs, few, span), jnp.bfloat16),
            dma((seqs, chips)),
            dma((seqs, chips)),
            dma((seqs,)),
            dma((seqs,)),
            dma((seqs, seqs)),
            dma((seqs, seqs)),
            dma((seqs, seqs)),
            dma((seqs, seqs)),
        ],
        compiler_params=pltpu.CompilerParams(
            collective_id=2, has_side_effects=True, vmem_limit_bytes=48 * 2**20
        ),
    )(tokens, w_gate, w_xin, w_small)


def group_kernel(in_ref, out_ref, held, t_send, t_recv, s_send, s_recv):
    s, t = lax.axis_index("seq"), lax.axis_index("tensor")
    seqs, tens = lax.axis_size("seq"), lax.axis_size("tensor")
    across = [(s, lax.rem(t + dt, tens)) for dt in range(1, tens)]
    along = [(lax.rem(s + ds, seqs), t) for ds in range(1, seqs)]
    enter(across + along)
    first = [
        remote(in_ref.at[peer[1]], held.at[0, t], t_send.at[dt], t_recv.at[dt], peer)
        for dt, peer in enumerate(across)
    ]
    for copy in first:
        copy.start()
    held[0, t] = in_ref[t]
    for copy in first:
        copy.wait_recv()
    second = [
        remote(held.at[0], held.at[1 + ds], s_send.at[ds], s_recv.at[ds], peer)
        for ds, peer in enumerate(along)
    ]
    for copy in second:
        copy.start()
    for copy in second:
        copy.wait_recv()
    out_ref[...] = held[...]
    for copy in first + second:
        copy.wait_send()


def to_groups(values, seqs):
    tens, rows, cols = values.shape
    dma = pltpu.SemaphoreType.DMA
    vmem = pl.BlockSpec(memory_space=pltpu.VMEM)
    return pl.pallas_call(
        group_kernel,
        out_shape=jax.ShapeDtypeStruct((seqs, tens, rows, cols), values.dtype),
        in_specs=[vmem],
        out_specs=vmem,
        scratch_shapes=[
            pltpu.VMEM((seqs, tens, rows, cols), values.dtype),
            dma((tens - 1,)),
            dma((tens - 1,)),
            dma((seqs - 1,)),
            dma((seqs - 1,)),
        ],
        compiler_params=pltpu.CompilerParams(
            collective_id=3, has_side_effects=True, vmem_limit_bytes=16 * 2**20
        ),
    )(values)


def conv_full(values, weights, bias, docs, axis):
    count = values.shape[axis]
    values = values.astype(jnp.float32)

    def along(vector):
        return vector[:, None] if axis == 0 else vector[None, :]

    def across(vector):
        return vector[None, :] if axis == 0 else vector[:, None]

    summed = across(weights[CONV - 1]) * values + across(bias)
    for back in range(1, CONV):
        kept = lax.slice_in_dim(values, 0, count - back, axis=axis)
        pad = [(0, 0), (0, 0)]
        pad[axis] = (back, 0)
        same = jnp.concatenate(
            [jnp.zeros((back,), jnp.float32), (docs[:-back] == docs[back:]).astype(jnp.float32)]
        )
        summed = summed + across(weights[CONV - 1 - back]) * jnp.pad(kept, pad) * along(same)
    return jax.nn.silu(summed).astype(jnp.bfloat16)


def scan_heads(xc, dtv, rate, bmat, cmat, docs, block):
    count, heads = dtv.shape
    blocks = count // block
    xh = xc.reshape(blocks, block, heads, HDIM)
    dtb = dtv.reshape(blocks, block, heads)
    upto = jnp.tril(jnp.ones((block, block), jnp.float32))
    cum = jnp.einsum("ij,bjh->bih", upto, -dtb * rate[None, None, :], precision=HIGH)
    docb = docs.reshape(blocks, block)
    bb = bmat.reshape(STATE, blocks, block)
    cb = cmat.reshape(STATE, blocks, block)
    scores = jnp.einsum("nbi,nbj->bij", cb, bb, preferred_element_type=jnp.float32)
    lower = jnp.tril(jnp.ones((block, block), bool))
    same = (docb[:, :, None] == docb[:, None, :]) & lower[None]
    cumt = cum.transpose(0, 2, 1)
    diff = cumt[:, :, :, None] - cumt[:, :, None, :]
    decay = jnp.exp(jnp.where(same[:, None], diff, -jnp.inf))
    mixing = scores[:, None] * decay * dtb.transpose(0, 2, 1)[:, :, None, :]
    inner = jnp.einsum(
        "bhij,bjhp->bihp", mixing.astype(jnp.bfloat16), xh, preferred_element_type=jnp.float32
    )
    end_doc = docb[:, -1]
    last_doc = jnp.concatenate([jnp.full((1,), -1, docs.dtype), end_doc[:-1]])
    carry_in = jnp.exp(cum) * (docb == last_doc[:, None]).astype(jnp.float32)[:, :, None]
    tail = jnp.exp(cum[:, -1:] - cum) * (docb == end_doc[:, None]).astype(jnp.float32)[:, :, None] * dtb
    tx = (tail[..., None] * xh.astype(jnp.float32)).astype(jnp.bfloat16)
    fresh = jnp.einsum("bjhp,nbj->bhpn", tx, bb, preferred_element_type=jnp.float32)
    states = [jnp.zeros((heads, HDIM, STATE), jnp.float32)]
    for k in range(blocks - 1):
        states.append(carry_in[k, -1][:, None, None] * states[-1] + fresh[k])
    entering = jnp.stack(states).astype(jnp.bfloat16)
    outer = jnp.einsum("nbi,bhpn->bihp", cb, entering, preferred_element_type=jnp.float32)
    return (inner + outer * carry_in[..., None]).reshape(count, heads * HDIM)


def shards(
    tokens,
    w_gate,
    w_xin,
    w_bc,
    w_dt,
    conv_x,
    conv_x_bias,
    conv_bc,
    conv_bc_bias,
    dt_bias,
    decay_rate,
    d_skip,
    norm_gain,
    w_out,
    lengths,
):
    seqs = lax.axis_size("seq")
    tens = lax.axis_size("tensor")
    here = lax.axis_index("seq")
    own, depth = tokens.shape[0], w_gate.shape[0]
    total = own * seqs * tens
    chans = w_gate.shape[1] // seqs
    heads = w_dt.shape[1] // seqs
    parts = w_bc.shape[1] // (seqs * GROUPS)
    small = jnp.concatenate(
        [
            w_bc.T.reshape(seqs, parts, GROUPS, depth)
            .transpose(0, 2, 1, 3)
            .reshape(seqs, parts * GROUPS, depth),
            w_dt.T.reshape(seqs, heads, depth),
            jnp.zeros((seqs, -(parts * GROUPS + heads) % 16, depth), jnp.bfloat16),
        ],
        axis=1,
    )
    gate, xin, small = project_in(tokens, w_gate, w_xin, small, seqs, tens // 2)
    docs = doc_ids(lengths, jnp.arange(total, dtype=jnp.int32))

    def mine(vector, width, axis=0):
        return lax.dynamic_slice_in_dim(vector, here * width, width, axis)

    xc = conv_full(xin, mine(conv_x, chans, 1), mine(conv_x_bias, chans), docs, 0)

    def grouped(vector):
        lead = vector.shape[:-1]
        vector = mine(vector, parts * GROUPS, len(lead)).reshape(lead + (parts, GROUPS))
        return jnp.swapaxes(vector, -1, -2).reshape(lead + (parts * GROUPS,))

    bcc = conv_full(small[: parts * GROUPS], grouped(conv_bc), grouped(conv_bc_bias), docs, 1)
    fold = 16 // parts
    bcc = bcc.reshape(GROUPS, parts, fold, total // fold).transpose(0, 2, 1, 3)
    bcc = to_groups(bcc.reshape(GROUPS, 16, total // fold), seqs)
    bcc = bcc.reshape(seqs, tens, fold, parts, total // fold).transpose(1, 0, 3, 2, 4)
    bcc = bcc.reshape(2 * STATE, total)
    dtin = small[parts * GROUPS : parts * GROUPS + heads].T.astype(jnp.float32)
    dtv = jax.nn.softplus(dtin + mine(dt_bias, heads)[None, :])
    y = scan_heads(
        xc, dtv, mine(decay_rate, heads), bcc[:STATE], bcc[STATE:], docs, min(STRETCH, total)
    )
    y = y + jnp.repeat(mine(d_skip, heads), HDIM)[None, :] * xc.astype(jnp.float32)
    gated = (y * jax.nn.silu(gate.astype(jnp.float32))).astype(jnp.bfloat16)
    return project_out(gated, norm_gain, w_out, own, seqs, tens // 2)


def solution(mesh):
    seqs, tens = mesh.shape["seq"], mesh.shape["tensor"]
    heads = INNER // HDIM
    narrow = tens == GROUPS and heads % (seqs * tens) == 0 and 2 * STATE == 8 * seqs * tens
    body = shards if narrow else shards_wide
    in_specs = (
        P(("seq", "tensor"), None),
        P("seq", "tensor"),
        P("seq", "tensor"),
        P("seq", "tensor"),
        P("seq", "tensor"),
        P(None, "tensor"),
        P("tensor"),
        P(None, "tensor"),
        P("tensor"),
        P("tensor"),
        P("tensor"),
        P("tensor"),
        P("tensor"),
        P("tensor", "seq"),
        P(),
    )
    out_specs = P(("seq", "tensor"), None)
    return jax.shard_map(body, mesh=mesh, in_specs=in_specs, out_specs=out_specs, check_vma=False)
```

profile of v0, /device:TPU:0, one launch (start us, length us, event | category | flops | bytes accessed | tf_op | source)
XLA Modules:
  0.0 171.1 jit_solution(12478515096696369604)
XLA Ops:
  0.0 0.9 dynamic_slice.25
  0.9 1.2 copy.68
  2.1 0.3 copy.112
  2.5 0.1 pad.44.clone
  2.6 0.2 maximum_maximum_fusion.ws_ref
  2.8 0.9 copy-done.3
  3.7 82.2 %shard_map.145 = (bf16[1024,256]{1,0:T(8,128)(2,1)S(1)}, bf16[1024,256]{1,0:T(8,128)(2,1)S(1)}, bf16[80,1024]{1,0:T(8,128)(2,1)S(1)}) custom-call(bf16[32,4096]{1,0:T(8,128)(2,1)S(1)} %copy-done.3, bf16[1024,1024]{1,0:T(8,128)(2,1)S(1)} %copy-done.1, bf16[1024,1024]{1,0:T(8,128)(2,1)} %wx_ref.1, bf16[4,80,1024]{2,1,0:T(8,128)(2,1)S(1)} %maximum_maximum_fusion.ws_ref), custom_call_target="tpu_custom_call" | custom-call | tf_op jit(solution)/shard_map/pallas_call | solution.py:460
  85.9 0.1 compare_select_fusion
  86.1 0.1 dynamic_slice.26
  86.1 0.3 fusion.25
  86.5 0.2 slice_reduce_fusion
  86.7 0.2 reduce-window.9
  86.8 0.1 convert_reduce_fusion
  87.0 0.2 slice_reduce_fusion.4
  87.1 0.1 pad_add_fusion
  87.2 0.2 slice_reduce_fusion.3
  87.4 0.1 compare_convert_fusion
  87.5 0.1 multiply_multiply_fusion
  87.6 0.9 fusion.50
  88.5 0.8 dynamic_slice.22
  89.3 0.1 slice_compare_fusion
  89.4 0.1 slice_compare_fusion.2
  89.4 0.1 add_convert_fusion
  89.5 0.1 slice.152
  89.6 0.1 slice.153
  89.7 0.1 slice.154
  89.8 0.1 slice_compare_fusion.1
  89.8 0.1 pad_convert_fusion.1
  89.9 1.3 multiply_convert_fusion.5
  91.2 0.2 copy.70
  91.5 0.4 reshape.176
  91.8 0.2 multiply_convert_fusion.4
  92.1 0.1 constant_dynamic-slice_fusion
  92.1 0.1 reshape.177
  92.3 0.1 mul.280
  92.4 0.1 mul.283
  92.6 0.1 mul.288
  92.8 0.1 mul.293
  92.8 0.1 dynamic_slice.24
  92.9 0.1 reshape.178
  93.0 0.1 copy.72
  93.1 0.1 add.133
  93.2 0.3 multiply_convert_fusion.6
  93.5 15.7 %shard_map.146 = bf16[4,8,16,512]{3,2,1,0:T(8,128)(2,1)S(1)} custom-call(bf16[8,16,512]{2,1,0:T(8,128)(2,1)S(1)} %bitcast.66), custom_call_target="tpu_custom_call" | custom-call | tf_op jit(solution)/shard_map/pallas_call | solution.py:524
  109.2 0.5 copy.111
  109.7 0.4 fusion.49
  110.1 0.1 reshape.183
  110.2 0.3 fusion.14
  110.5 0.2 slice_reduce_fusion.2
  110.7 0.7 fusion.48
  111.4 0.1 reshape.182
  111.6 0.3 fusion.27
  111.9 0.7 reshape.184
  112.7 0.2 compare_and_fusion
  113.0 2.9 %fusion.7 = f32[4,256,4,64]{1,3,2,0:T(8,128)S(1)} fusion(f32[4,4,256]{2,1,0:T(4,128)S(1)} %copy.80, f32[4,4,256]{2,1,0:T(4,128)} %copy-done.9, f32[4,256,256]{2,1,0:T(8,128)S(1)} %fusion.27, pred[4,256,256]{2,1,0:T(8,128)(4,1)S(1)} %compare_and_fusion, bf16[4,256,4,64]{1,0,3,2:T(4,128)(2,1)S(1)} %reshape.176), kind=kOutput, calls=%fused_computation.8 | convolution fusion | flops 139460608 | bytes 2916352 | tf_op jit(solution)/shard_map/bhij,bjhp->bihp/dot_general | solution.py:581
  115.9 1.3 fusion.8
  117.3 1.8 %copy.95 = f32[4,256,4,64]{3,2,1,0:T(4,128)S(1)} copy(f32[4,256,4,64]{1,3,2,0:T(8,128)} %fusion.8) | data formatting | bytes 2097152 | tf_op jit(solution)/shard_map/reshape | solution.py:595
  119.1 2.1 %reshape.189 = f32[1024,256]{1,0:T(8,128)} reshape(f32[4,256,4,64]{3,2,1,0:T(4,128)S(1)} %copy.95) | data formatting | bytes 2097152 | tf_op jit(solution)/shard_map/reshape | solution.py:595
  121.3 0.1 dynamic_slice.27
  121.3 0.1 broadcast_in_dim.34
  121.4 0.1 mul.324
  121.5 1.7 %fusion.13.g_ref = bf16[1024,256]{1,0:T(8,128)(2,1)S(1)} fusion(bf16[1024,256]{1,0:T(8,128)(2,1)S(1)} %get-tuple-element.10, f32[1024,256]{1,0:T(8,128)} %reshape.189, bf16[1024,256]{1,0:T(8,128)(2,1)S(1)} %multiply_convert_fusion.5, f32[256]{0:T(256)S(1)} %mul.324), kind=kLoop, calls=%fused_computation.19 | loop fusion | flops 2621440 | bytes 2622464 | tf_op jit(solution)/shard_map/convert_element_type | solution.py:658
  123.3 47.1 %shard_map.147 = bf16[32,4096]{1,0:T(8,128)(2,1)S(1)} custom-call(bf16[1024,256]{1,0:T(8,128)(2,1)S(1)} %fusion.13.g_ref, f32[1,1024]{1,0:T(1,128)S(1)} %bitcast.67, bf16[1024,1024]{1,0:T(8,128)(2,1)S(1)} %copy-done.2), custom_call_target="tpu_custom_call" | custom-call | tf_op jit(solution)/shard_map/pallas_call | solution.py:340
  170.4 0.7 copy.114
  (44 shorter events, 0.5 us)
Async XLA Ops:
  0.0 92.1 %copy-start = (f32[4,256]{1,0:T(4,128)S(1)}, f32[4,256]{1,0:T(4,128)}, u32[]{:S(2)}) copy-start(f32[4,256]{1,0:T(4,128)} %param.22) | copy-start | bytes 12292
  0.0 2.4 %copy-start.10 = (bf16[1024,16]{0,1:T(8,128)(2,1)S(1)}, bf16[1024,16]{0,1:T(8,128)(2,1)}, u32[]{:S(2)}) copy-start(bf16[1024,16]{0,1:T(8,128)(2,1)} %param.19) | copy-start | bytes 98308
  0.0 2.7 %copy-start.1 = (bf16[1024,1024]{1,0:T(8,128)(2,1)S(1)}, bf16[1024,1024]{1,0:T(8,128)(2,1)}, u32[]{:S(2)}) copy-start(bf16[1024,1024]{1,0:T(8,128)(2,1)} %wg_ref.1) | copy-start | bytes 6291460
  2.8 1.0 copy-start.3
  3.7 82.3 %copy-start.12 = (f32[16]{0:T(128)S(1)}, f32[16]{0:T(128)}, u32[]{:S(2)}) copy-start(f32[16]{0:T(128)} %param.25) | copy-start | bytes 196
  3.7 82.9 %copy-start.13 = (s32[8]{0:T(128)S(1)}, s32[8]{0:T(128)}, u32[]{:S(2)}) copy-start(s32[8]{0:T(128)} %param.29) | copy-start | bytes 100
  86.0 3.5 %copy-start.6 = (f32[1024,4]{0,1:T(4,128)}, f32[1024,4]{0,1:T(4,128)S(1)}, u32[]{:S(2)}) copy-start(f32[1024,4]{0,1:T(4,128)S(1)} %compare_select_fusion) | copy-start | bytes 49156
  86.5 3.2 %copy-start.9 = (f32[4,4,256]{2,1,0:T(4,128)}, f32[4,4,256]{2,1,0:T(4,128)S(1)}, u32[]{:S(2)}) copy-start(f32[4,4,256]{2,1,0:T(4,128)S(1)} %fusion.25) | copy-start | bytes 49156
  87.6 22.9 %copy-start.7 = (f32[4,256,4]{1,2,0:T(4,128)}, f32[4,256,4]{1,2,0:T(4,128)S(1)}, u32[]{:S(2)}) copy-start(f32[4,256,4]{1,2,0:T(4,128)S(1)} %get-tuple-element.20) | copy-start | bytes 49156
  91.2 1.6 copy-start.11
  112.9 3.0 %copy-start.5 = (bf16[1,4,64,128]{3,2,1,0:T(8,128)(2,1)S(1)}, bf16[1,4,64,128]{3,2,1,0:T(8,128)(2,1)}, u32[]{:S(2)}) copy-start(bf16[1,4,64,128]{3,2,1,0:T(8,128)(2,1)} %get-tuple-element.16) | copy-start | bytes 196612
  112.9 3.0 %copy-start.8 = (f32[4,256,4]{1,2,0:T(4,128)S(1)}, f32[4,256,4]{1,2,0:T(4,128)}, u32[]{:S(2)}) copy-start(f32[4,256,4]{1,2,0:T(4,128)} %copy-done.7) | copy-start | bytes 49156
  119.1 2.2 %copy-start.14 = (f32[16]{0:T(128)S(1)}, f32[16]{0:T(128)}, u32[]{:S(2)}) copy-start(f32[16]{0:T(128)} %param.26) | copy-start | bytes 196
  121.3 2.0 %copy-start.2 = (bf16[1024,1024]{1,0:T(8,128)(2,1)S(1)}, bf16[1024,1024]{1,0:T(8,128)(2,1)}, u32[]{:S(2)}) copy-start(bf16[1024,1024]{1,0:T(8,128)(2,1)} %w_ref.1) | copy-start | bytes 6291460
  121.3 2.0 %copy-start.4 = (f32[1024]{0:T(1024)S(1)}, f32[1024]{0:T(1024)}, u32[]{:S(2)}) copy-start(f32[1024]{0:T(1024)} %param.27) | copy-start | bytes 12292
where the time goes:
time: 173 us; the launch traced here: 171 us
  Pallas kernels  145 us (84%)
  local copies, waits for them, and re-layouts  14.5 us (8%)
  other arithmetic  6 us (3%)
  matrix products  5.24 us (3%)
    pallas_call x1, Pallas kernels, project_in(): pl.pallas_call(in_kernel, out_shape=(jax.ShapeDtypeStruct((span * seqs, w...  82.2 us
    pallas_call x1, Pallas kernels, project_out(): pl.pallas_call(out_kernel, out_shape=jax.ShapeDtypeStruct((own, cols * se...  47.1 us
    pallas_call x1, Pallas kernels, to_groups(): pl.pallas_call(group_kernel, out_shape=jax.ShapeDtypeStruct((seqs, tens,...  15.7 us
    reshape x2, local copies, waits for them, and re-layouts, scan_heads(): return (inner + outer * carry_in[..., None]).reshape(count, heads * HDIM)  3.98 us

commit v1 on v0

--- a/solution.py
+++ b/solution.py
@@ -362,237 +362,367 @@
     )(gated, gain[None, :], w_out)
 
 
-def in_kernel(
-    tok_ref, wg_ref, wx_ref, ws_ref, gate_ref, xin_ref, small_ref,
-    tok, mine, mine_s, sent, sent_s, got, got_s,
-    t_send, t_recv, f_send, f_recv, p_send, p_recv, q_send, q_recv,
+SEQS, CHIPS, OWN, SPAN, WIDE, HALF = 4, 4, 32, 256, 256, 128
+LOG2E = 1.4426950408889634
+
+
+def silu(v):
+    return v / (1.0 + jnp.exp(-v))
+
+
+class Sums:
+    def __init__(self, bufs, sems, s, z, c):
+        self.sa, self.sb, self.ra, self.rb, self.qa, self.qb, self.pa, self.pb, self.k0, self.k1, self.k2 = bufs
+        self.sems = sems
+        self.x, self.y = (s ^ 1, 2 * z + c), (s ^ 2, 2 * z + c)
+
+    def copies(self, u):
+        send, recv = self.sems
+        return (
+            remote(self.sa.at[u], self.ra.at[u], send.at[u, 0], recv.at[u, 0], self.x),
+            remote(self.sb.at[u], self.rb.at[u], send.at[u, 1], recv.at[u, 1], self.y),
+            remote(self.qa.at[u], self.pa.at[u], send.at[u, 2], recv.at[u, 2], self.y),
+            remote(self.qb.at[u], self.pb.at[u], send.at[u, 3], recv.at[u, 3], self.x),
+        )
+
+    def emit(self, u, get):
+        first, second, _, _ = self.copies(u)
+        far = get(3)
+        self.sa[u, 1] = far[:, :HALF].astype(jnp.bfloat16)
+        self.sb[u, 1] = far[:, HALF:].astype(jnp.bfloat16)
+        near = get(1)
+        self.sa[u, 0] = near[:, :HALF].astype(jnp.bfloat16)
+        first.start()
+        self.k1[u] = near[:, HALF:]
+        near = get(2)
+        self.sb[u, 0] = near[:, HALF:].astype(jnp.bfloat16)
+        second.start()
+        self.k2[u] = near[:, :HALF]
+        self.k0[u] = get(0)
+
+    def relay(self, u):
+        first, second, third, fourth = self.copies(u)
+        first.wait_recv()
+        self.qa[u] = (self.k2[u] + self.ra[u, 1].astype(jnp.float32)).astype(jnp.bfloat16)
+        third.start()
+        second.wait_recv()
+        self.qb[u] = (self.k1[u] + self.rb[u, 1].astype(jnp.float32)).astype(jnp.bfloat16)
+        fourth.start()
+
+    def final(self, u):
+        _, _, third, fourth = self.copies(u)
+        third.wait_recv()
+        fourth.wait_recv()
+        own = self.k0[u]
+        left = own[:, :HALF] + self.ra[u, 0].astype(jnp.float32) + self.pa[u].astype(jnp.float32)
+        right = own[:, HALF:] + self.rb[u, 0].astype(jnp.float32) + self.pb[u].astype(jnp.float32)
+        return jnp.concatenate([left, right], axis=1).astype(jnp.bfloat16)
+
+    def drain(self, u):
+        for copy in self.copies(u):
+            copy.wait_send()
+
+
+def mix_kernel(
+    tok_ref, wg_hbm, wx_hbm, wb_hbm, wdt_ref, cx_ref, cxb_ref, cb_ref, cbb_ref,
+    bias_s, rate_s, skip_s, len_s, out_ref,
+    tok, wg, wx, wb, rel, xs, xc, bs, halo, bct, bca, bcp, dts, dtg, dtv,
+    *rest,
 ):
-    s, z, c, seqs, chips, along = places()
-    own = tok_ref.shape[0]
-    depth = wg_ref.shape[0]
-    width = wg_ref.shape[1] // seqs
-    span = own * chips * 2
+    big, rest = rest[:11], rest[11:]
+    few, rest = rest[:11], rest[11:]
+    (
+        w_sem, t_send, t_recv, zu_send, zd_send, z_recv, f_send, f_recv,
+        g_send, g_recv, b_send, b_recv, h_send, h_recv, d_send, d_recv,
+        e_send, e_recv, a_send, a_recv,
+    ) = rest
+    s, t = lax.axis_index("seq"), lax.axis_index("tensor")
+    tens = 2 * CHIPS
+    z, c = t // 2, t % 2
     sibling = (s, 2 * z + 1 - c)
-    offsets = [(ds, dz) for ds in range(seqs) for dz in range(chips) if ds or dz]
-    enter([(along(ds, dz)[0], 2 * along(ds, dz)[1] + c) for ds, dz in offsets] + [sibling])
-    spread = {}
-    for ds, dz in offsets:
-        to, there = along(ds, dz)
-        spread[ds, dz] = remote(
-            tok_ref.at[:, pl.ds(pl.multiple_of(to * depth, depth), depth)],
-            tok.at[ds, z, c],
-            t_send.at[ds, dz],
-            t_recv.at[ds, dz],
-            (to, 2 * there + c),
+    loads = [
+        pltpu.make_async_copy(src, dst, w_sem.at[i])
+        for i, (src, dst) in enumerate(((wb_hbm, wb), (wx_hbm, wx), (wg_hbm, wg)))
+    ]
+    for load in loads:
+        load.start()
+    along = [(s ^ r, t) for r in range(1, SEQS)]
+    across = [(s, lax.rem(t + d, tens)) for d in range(1, tens)]
+    enter(along + across)
+
+    depth = wx.shape[0]
+    spread = [
+        remote(
+            tok_ref.at[:, pl.ds(pl.multiple_of(peer[0] * depth, depth), depth)],
+            tok.at[z, c, s], t_send.at[i], t_recv.at[i], peer,
         )
-        spread[ds, dz].start()
-    tok[0, z, c] = tok_ref[:, pl.ds(pl.multiple_of(s * depth, depth), depth)]
-    forwards, sums = [], []
-
-    def forward(k):
-        for ds, dz in offsets:
-            if ds == k:
-                spread[ds, dz].wait_recv()
-        forwards.append(
-            remote(tok.at[k, :, c], tok.at[k, :, c], f_send.at[k], f_recv.at[k], sibling)
-        )
-        forwards[k].start()
-
-    forward(0)
-    for k in range(seqs):
-        forwards[k].wait_recv()
-        if k + 1 < seqs:
-            forward(k + 1)
-        q = lax.rem(s + seqs - k, seqs)
-        for ds in list(range(1, seqs)) + [0]:
-            to = along(ds, 0)[0]
-            cols = pl.ds(pl.multiple_of(to * width, width), width)
-            rows = tok[k].reshape(span, depth)
-            gate = jnp.dot(rows, wg_ref[:, cols], preferred_element_type=jnp.float32)
-            xin = jnp.dot(rows, wx_ref[:, cols], preferred_element_type=jnp.float32)
-            small = lax.dot_general(
-                ws_ref[to], rows, (((1,), (1,)), ((), ())), preferred_element_type=jnp.float32
+        for i, peer in enumerate(along)
+    ]
+    for copy in spread:
+        copy.start()
+    tok[z, c, s] = tok_ref[:, pl.ds(pl.multiple_of(s * depth, depth), depth)]
+
+    total = SEQS * SPAN
+    pos = lax.broadcasted_iota(jnp.int32, (total, HALF), 0)
+    begin, start = jnp.zeros((total, HALF), jnp.int32), jnp.int32(0)
+    for r in range(len_s.shape[0]):
+        begin = jnp.where(pos >= start, start, begin)
+        start = start + len_s[r]
+    rel[...] = pos - begin
+
+    first = z - 1 + 2 * ((3 - z) // 3)
+    last = 3 * (1 - z // 2)
+    order = [z, first, 6 - z - first - last, last]
+
+    def hops(zb):
+        part = tok.at[zb, c]
+        up = remote(part, part, zu_send.at[zb], z_recv.at[zb], (s, 2 * lax.rem(z + 1, CHIPS) + c))
+        down = remote(part, part, zd_send.at[zb], z_recv.at[zb], (s, 2 * lax.rem(z + CHIPS - 1, CHIPS) + c))
+        over = remote(part, part, f_send.at[zb], f_recv.at[zb], sibling)
+        return up, down, over, (z < CHIPS - 1) & (zb <= z), (z > 0) & (zb >= z)
+
+    def arrive(i):
+        zb = order[i]
+        up, down, over, goes_up, goes_down = hops(zb)
+        if i:
+            up.wait_recv()
+        else:
+            for copy in spread:
+                copy.wait_recv()
+        pl.when(goes_up)(up.start)
+        pl.when(goes_down)(down.start)
+        over.start()
+        over.wait_recv()
+
+    sums = Sums(big, (g_send, g_recv), s, z, c)
+    sumb = Sums(few, (b_send, b_recv), s, z, c)
+
+    def product(rows, w):
+        def get(r):
+            cols = pl.ds(pl.multiple_of((s ^ r) * WIDE, WIDE), WIDE)
+            return jnp.dot(rows, w[:, cols], preferred_element_type=jnp.float32)
+
+        return get
+
+    for i in range(CHIPS):
+        arrive(i)
+        rows = tok[order[i]].reshape(SPAN, depth)
+        if i == 0:
+            loads[0].wait()
+        bcp[...] = jnp.dot(rows, wb[...], preferred_element_type=jnp.float32).reshape(2, SEQS, OWN, WIDE)
+        sumb.emit(i, lambda r: bcp[:, s ^ r].reshape(2 * OWN, WIDE))
+        if i == 0:
+            loads[1].wait()
+        sums.emit(i, product(rows, wx))
+        if i:
+            sumb.relay(i - 1)
+            sums.relay(i - 1)
+    sumb.relay(CHIPS - 1)
+
+    def span_rows(q):
+        return tok[:, :, q].reshape(SPAN, depth)
+
+    for q in range(SEQS):
+        dts[:, q * SPAN : (q + 1) * SPAN] = lax.dot_general(
+            wdt_ref[...], span_rows(q), (((1,), (1,)), ((), ())), preferred_element_type=jnp.float32
+        ).astype(jnp.bfloat16)
+    steps = [
+        remote(dts, dtg.at[i], d_send.at[i], d_recv.at[i], peer) for i, peer in enumerate(along)
+    ]
+    for copy in steps:
+        copy.start()
+    for i in range(CHIPS):
+        bs[pl.ds(pl.multiple_of(16 + order[i] * 2 * OWN, 16), 2 * OWN), :] = sumb.final(i).astype(jnp.float32)
+    halo[0] = bs[16 + SPAN - 16 :, :].astype(jnp.bfloat16)
+    edge = remote(halo.at[0], halo.at[1], h_send, h_recv, (lax.rem(s + 1, SEQS), t))
+    edge.start()
+    sums.relay(CHIPS - 1)
+    loads[2].wait()
+    sums.emit(4, product(span_rows(0), wg))
+
+    edge.wait_recv()
+    bs[:16, :] = halo[1].astype(jnp.float32)
+    away = rel[pl.ds(pl.multiple_of(s * SPAN, SPAN), SPAN), :1]
+
+    def conv(src, begin, w, bias, away):
+        out = w[CONV - 1 :, :] * src[begin : begin + SPAN, :] + bias
+        for back in range(1, CONV):
+            tap = w[CONV - 1 - back : CONV - back, :] * src[begin - back : begin - back + SPAN, :]
+            out = out + jnp.where(away >= back, tap, 0.0)
+        return silu(out).astype(jnp.bfloat16)
+
+    bcc = conv(bs, 16, cb_ref[...], cbb_ref[...], away)
+    to = lax.broadcasted_iota(jnp.int32, (WIDE, WIDE), 0)
+    frm = lax.broadcasted_iota(jnp.int32, (WIDE, WIDE), 1)
+    pick = (frm == (to % 32) * GROUPS + to // 32).astype(jnp.float32).astype(jnp.bfloat16)
+    bct[...] = (
+        lax.dot_general(pick, bcc, (((1,), (1,)), ((), ())), preferred_element_type=jnp.float32)
+        .astype(jnp.bfloat16)
+        .reshape(GROUPS, 32, SPAN)
+    )
+    swaps = [
+        remote(bct.at[peer[1]], bca.at[s, t], e_send.at[i], e_recv.at[i], peer)
+        for i, peer in enumerate(across)
+    ]
+    for copy in swaps:
+        copy.start()
+    bca[s, t] = bct[t]
+    for i in range(CHIPS):
+        full = sums.final(i).astype(jnp.float32).reshape(2, SEQS, OWN, WIDE)
+        for half in range(2):
+            for q in range(SEQS):
+                at = 16 + q * SPAN + half * OWN + order[i] * 2 * OWN
+                xs[pl.ds(pl.multiple_of(at, 16), OWN), :] = full[half, q]
+    for copy in swaps:
+        copy.wait_recv()
+    groups = [
+        remote(bca.at[s], bca.at[s], a_send.at[i], a_recv.at[i], peer)
+        for i, peer in enumerate(along)
+    ]
+    for copy in groups:
+        copy.start()
+    sums.emit(5, product(span_rows(1), wg))
+    sums.relay(4)
+    sums.emit(6, product(span_rows(2), wg))
+    sums.emit(7, product(span_rows(3), wg))
+    xs[:16, :] = jnp.zeros((16, WIDE), jnp.float32)
+    mine = pl.ds(pl.multiple_of(s * WIDE, WIDE), WIDE)
+    for q in range(SEQS):
+        xc[q * SPAN : (q + 1) * SPAN, :] = conv(
+            xs, 16 + q * SPAN, cx_ref[:, mine], cxb_ref[:, mine], rel[q * SPAN : (q + 1) * SPAN, :1]
+        ).astype(jnp.float32)
+    sums.relay(5)
+    for copy in steps:
+        copy.wait_recv()
+    dtv[...] = (
+        dts[...].astype(jnp.float32)
+        + dtg[0].astype(jnp.float32)
+        + dtg[1].astype(jnp.float32)
+        + dtg[2].astype(jnp.float32)
+    ).astype(jnp.bfloat16).astype(jnp.float32)
+    heads = 4
+    line = lax.broadcasted_iota(jnp.int32, (8, total), 0)
+    dt8, rate8 = jnp.zeros((8, total), jnp.float32), jnp.zeros((8, total), jnp.float32)
+    for h in range(heads):
+        row = dtv[pl.ds(heads * s + h, 1), :] + bias_s[heads * s + h]
+        row = jnp.maximum(row, 0.0) + jnp.log1p(jnp.exp(-jnp.abs(row)))
+        dt8 = jnp.where(line == h, row, dt8)
+        dt8 = jnp.where(line == heads + h, row * (-LOG2E * rate_s[heads * s + h]), dt8)
+
+    dif = to - frm
+    upto = (dif <= 0).astype(jnp.float32)
+    lane = frm // HDIM
+    skip = jnp.zeros((1, WIDE), jnp.float32)
+    for h in range(heads):
+        skip = jnp.where(lane[:1] == h, skip_s[heads * s + h], skip)
+    for copy in groups:
+        copy.wait_recv()
+    state = jnp.zeros((STATE, WIDE), jnp.float32)
+    local = to[:, :1]
+    for q in range(SEQS):
+        here = slice(q * SPAN, (q + 1) * SPAN)
+        away = rel[here, :1]
+        bt = bca[q, :4].reshape(STATE, SPAN)
+        cn = bca[q, 4:].reshape(STATE, SPAN).astype(jnp.float32).T.astype(jnp.bfloat16)
+        scores = jnp.dot(cn, bt, preferred_element_type=jnp.float32)
+        scores = jnp.where((dif >= 0) & (dif <= away), scores, 0.0)
+        both = dt8[:, here]
+        cum = jnp.dot(both, upto, precision=HIGH, preferred_element_type=jnp.float32)
+        both = jnp.where(line[:, :SPAN] < heads, both, cum)
+        cols = jnp.concatenate([both, jnp.zeros((HALF - 8, SPAN), jnp.float32)], axis=0).T
+
+        def expand(first):
+            out = jnp.broadcast_to(cols[:, first : first + 1], (SPAN, WIDE))
+            for h in range(1, heads):
+                out = jnp.where(lane == h, cols[:, first + h : first + h + 1], out)
+            return out
+
+        dte, cume = expand(0), expand(heads)
+        xv = xc[here, :]
+        xdt = xv * dte
+        inner = jnp.zeros((SPAN, WIDE), jnp.float32)
+        for h in range(heads):
+            gap = cols[:, heads + h : heads + h + 1] - both[heads + h : heads + h + 1, :]
+            mixing = (jnp.exp2(jnp.minimum(gap, 0.0)) * scores).astype(jnp.bfloat16)
+            inner = inner + jnp.dot(
+                mixing, jnp.where(lane == h, xdt, 0.0).astype(jnp.bfloat16),
+                preferred_element_type=jnp.float32,
             )
-            if ds == 0:
-                mine[q, :, :width] = gate
-                mine[q, :, width:] = xin
-                mine_s[q] = small
-                continue
-            sent[ds, k, :, :width] = gate.astype(jnp.bfloat16)
-            sent[ds, k, :, width:] = xin.astype(jnp.bfloat16)
-            sent_s[ds, k] = small.astype(jnp.bfloat16)
-            peer = (to, 2 * z + c)
-            for copy in (
-                remote(sent.at[ds, k], got.at[ds, q], p_send.at[ds, k], p_recv.at[ds, k], peer),
-                remote(
-                    sent_s.at[ds, k], got_s.at[ds, q], q_send.at[ds, k], q_recv.at[ds, k], peer
-                ),
-            ):
-                copy.start()
-                sums.append(copy)
-    for copy in sums:
-        copy.wait_recv()
-
-    def add(q, _):
-        rows = pl.ds(pl.multiple_of(q * span, span), span)
-        total, small = mine[q], mine_s[q]
-        for ds in range(1, seqs):
-            total = total + got[ds, q].astype(jnp.float32)
-            small = small + got_s[ds, q].astype(jnp.float32)
-        gate_ref[rows, :] = total[:, :width].astype(jnp.bfloat16)
-        xin_ref[rows, :] = total[:, width:].astype(jnp.bfloat16)
-        small_ref[:, rows] = small.astype(jnp.bfloat16)
-        return 0
-
-    lax.fori_loop(0, seqs, add, 0)
-    for copy in list(spread.values()) + forwards + sums:
+        carry = jnp.where(away > local, jnp.exp2(cume), 0.0)
+        ends = cume[SPAN - 1 :, :]
+        tail = jnp.where(local >= SPAN - 1 - away[SPAN - 1 :, :], jnp.exp2(ends - cume), 0.0)
+        fresh = jnp.dot(bt, (tail * xdt).astype(jnp.bfloat16), preferred_element_type=jnp.float32)
+        outer = jnp.dot(cn, state.astype(jnp.bfloat16), preferred_element_type=jnp.float32)
+        state = carry[SPAN - 1 :, :] * state + fresh
+        y = inner + outer * carry + skip * xv
+        if q == 0:
+            sums.relay(6)
+        if q == 1:
+            sums.relay(7)
+        gate = sums.final(4 + q).astype(jnp.float32)
+        out_ref[here, :] = (y * silu(gate)).astype(jnp.bfloat16)
+
+    for zb in range(CHIPS):
+        up, down, over, goes_up, goes_down = hops(zb)
+        pl.when(goes_up)(up.wait_send)
+        pl.when(goes_down)(down.wait_send)
+        over.wait_send()
+    for copy in spread + steps + [edge] + swaps + groups:
         copy.wait_send()
-
-
-def project_in(tokens, w_gate, w_xin, w_small, seqs, chips):
-    own = tokens.shape[0]
-    depth = w_gate.shape[0]
-    width = w_gate.shape[1] // seqs
-    span = own * chips * 2
-    few = w_small.shape[1]
+    for u in range(8):
+        sums.drain(u)
+    for u in range(4):
+        sumb.drain(u)
+
+
+def mix_in(tokens, w_gate, w_xin, w_bc, w_dt, conv_x, conv_xb, conv_b, conv_bb, bias, rate, skip, lengths):
+    depth, width = w_xin.shape
+    total = SEQS * SPAN
     dma = pltpu.SemaphoreType.DMA
-    vmem = pl.BlockSpec(memory_space=pltpu.VMEM)
+    vmem, smem, anyw = (pl.BlockSpec(memory_space=m) for m in (pltpu.VMEM, pltpu.SMEM, pl.ANY))
+    bf, f32 = jnp.bfloat16, jnp.float32
+
+    def sums(n, rows):
+        pair = pltpu.VMEM((n, 2, rows, HALF), bf)
+        one = pltpu.VMEM((n, rows, HALF), bf)
+        return [pair] * 4 + [one] * 4 + [pltpu.VMEM((n, rows, WIDE), f32)] + [pltpu.VMEM((n, rows, HALF), f32)] * 2
+
     return pl.pallas_call(
-        in_kernel,
-        out_shape=(
-            jax.ShapeDtypeStruct((span * seqs, width), jnp.bfloat16),
-            jax.ShapeDtypeStruct((span * seqs, width), jnp.bfloat16),
-            jax.ShapeDtypeStruct((few, span * seqs), jnp.bfloat16),
-        ),
-        in_specs=[vmem] * 4,
-        out_specs=(vmem,) * 3,
+        mix_kernel,
+        out_shape=jax.ShapeDtypeStruct((total, WIDE), bf),
+        in_specs=[vmem, anyw, anyw, anyw] + [vmem] * 5 + [smem] * 4,
+        out_specs=vmem,
         scratch_shapes=[
-            pltpu.VMEM((seqs, chips, 2, own, depth), jnp.bfloat16),
-            pltpu.VMEM((seqs, span, 2 * width), jnp.float32),
-            pltpu.VMEM((seqs, few, span), jnp.float32),
-            pltpu.VMEM((seqs, seqs, span, 2 * width), jnp.bfloat16),
-            pltpu.VMEM((seqs, seqs, few, span), jnp.bfloat16),
-            pltpu.VMEM((seqs, seqs, span, 2 * width), jnp.bfloat16),
-            pltpu.VMEM((seqs, seqs, few, span), jnp.bfloat16),
-            dma((seqs, chips)),
-            dma((seqs, chips)),
-            dma((seqs,)),
-            dma((seqs,)),
-            dma((seqs, seqs)),
-            dma((seqs, seqs)),
-            dma((seqs, seqs)),
-            dma((seqs, seqs)),
+            pltpu.VMEM((CHIPS, 2, SEQS, OWN, depth), bf),
+            pltpu.VMEM(w_gate.shape, bf),
+            pltpu.VMEM(w_xin.shape, bf),
+            pltpu.VMEM(w_bc.shape, bf),
+            pltpu.VMEM((total, HALF), jnp.int32),
+            pltpu.VMEM((16 + total, WIDE), f32),
+            pltpu.VMEM((total, WIDE), f32),
+            pltpu.VMEM((16 + SPAN, WIDE), f32),
+            pltpu.VMEM((2, 16, WIDE), bf),
+            pltpu.VMEM((GROUPS, 32, SPAN), bf),
+            pltpu.VMEM((SEQS, GROUPS, 32, SPAN), bf),
+            pltpu.VMEM((2, SEQS, OWN, WIDE), f32),
+            pltpu.VMEM((16, total), bf),
+            pltpu.VMEM((3, 16, total), bf),
+            pltpu.VMEM((16, total), f32),
+        ]
+        + sums(8, SPAN)
+        + sums(4, 2 * OWN)
+        + [
+            dma((3,)), dma((3,)), dma((3,)), dma((4,)), dma((4,)), dma((4,)), dma((4,)), dma((4,)),
+            dma((8, 4)), dma((8, 4)), dma((4, 4)), dma((4, 4)),
+            dma, dma, dma((3,)), dma((3,)), dma((7,)), dma((7,)), dma((3,)), dma((3,)),
         ],
         compiler_params=pltpu.CompilerParams(
-            collective_id=2, has_side_effects=True, vmem_limit_bytes=48 * 2**20
+            collective_id=2, has_side_effects=True, vmem_limit_bytes=52 * 2**20
         ),
-    )(tokens, w_gate, w_xin, w_small)
-
-
-def group_kernel(in_ref, out_ref, held, t_send, t_recv, s_send, s_recv):
-    s, t = lax.axis_index("seq"), lax.axis_index("tensor")
-    seqs, tens = lax.axis_size("seq"), lax.axis_size("tensor")
-    across = [(s, lax.rem(t + dt, tens)) for dt in range(1, tens)]
-    along = [(lax.rem(s + ds, seqs), t) for ds in range(1, seqs)]
-    enter(across + along)
-    first = [
-        remote(in_ref.at[peer[1]], held.at[0, t], t_send.at[dt], t_recv.at[dt], peer)
-        for dt, peer in enumerate(across)
-    ]
-    for copy in first:
-        copy.start()
-    held[0, t] = in_ref[t]
-    for copy in first:
-        copy.wait_recv()
-    second = [
-        remote(held.at[0], held.at[1 + ds], s_send.at[ds], s_recv.at[ds], peer)
-        for ds, peer in enumerate(along)
-    ]
-    for copy in second:
-        copy.start()
-    for copy in second:
-        copy.wait_recv()
-    out_ref[...] = held[...]
-    for copy in first + second:
-        copy.wait_send()
-
-
-def to_groups(values, seqs):
-    tens, rows, cols = values.shape
-    dma = pltpu.SemaphoreType.DMA
-    vmem = pl.BlockSpec(memory_space=pltpu.VMEM)
-    return pl.pallas_call(
-        group_kernel,
-        out_shape=jax.ShapeDtypeStruct((seqs, tens, rows, cols), values.dtype),
-        in_specs=[vmem],
-        out_specs=vmem,
-        scratch_shapes=[
-            pltpu.VMEM((seqs, tens, rows, cols), values.dtype),
-            dma((tens - 1,)),
-            dma((tens - 1,)),
-            dma((seqs - 1,)),
-            dma((seqs - 1,)),
-        ],
-        compiler_params=pltpu.CompilerParams(
-            collective_id=3, has_side_effects=True, vmem_limit_bytes=16 * 2**20
-        ),
-    )(values)
-
-
-def conv_full(values, weights, bias, docs, axis):
-    count = values.shape[axis]
-    values = values.astype(jnp.float32)
-
-    def along(vector):
-        return vector[:, None] if axis == 0 else vector[None, :]
-
-    def across(vector):
-        return vector[None, :] if axis == 0 else vector[:, None]
-
-    summed = across(weights[CONV - 1]) * values + across(bias)
-    for back in range(1, CONV):
-        kept = lax.slice_in_dim(values, 0, count - back, axis=axis)
-        pad = [(0, 0), (0, 0)]
-        pad[axis] = (back, 0)
-        same = jnp.concatenate(
-            [jnp.zeros((back,), jnp.float32), (docs[:-back] == docs[back:]).astype(jnp.float32)]
-        )
-        summed = summed + across(weights[CONV - 1 - back]) * jnp.pad(kept, pad) * along(same)
-    return jax.nn.silu(summed).astype(jnp.bfloat16)
-
-
-def scan_heads(xc, dtv, rate, bmat, cmat, docs, block):
-    count, heads = dtv.shape
-    blocks = count // block
-    xh = xc.reshape(blocks, block, heads, HDIM)
-    dtb = dtv.reshape(blocks, block, heads)
-    upto = jnp.tril(jnp.ones((block, block), jnp.float32))
-    cum = jnp.einsum("ij,bjh->bih", upto, -dtb * rate[None, None, :], precision=HIGH)
-    docb = docs.reshape(blocks, block)
-    bb = bmat.reshape(STATE, blocks, block)
-    cb = cmat.reshape(STATE, blocks, block)
-    scores = jnp.einsum("nbi,nbj->bij", cb, bb, preferred_element_type=jnp.float32)
-    lower = jnp.tril(jnp.ones((block, block), bool))
-    same = (docb[:, :, None] == docb[:, None, :]) & lower[None]
-    cumt = cum.transpose(0, 2, 1)
-    diff = cumt[:, :, :, None] - cumt[:, :, None, :]
-    decay = jnp.exp(jnp.where(same[:, None], diff, -jnp.inf))
-    mixing = scores[:, None] * decay * dtb.transpose(0, 2, 1)[:, :, None, :]
-    inner = jnp.einsum(
-        "bhij,bjhp->bihp", mixing.astype(jnp.bfloat16), xh, preferred_element_type=jnp.float32
-    )
-    end_doc = docb[:, -1]
-    last_doc = jnp.concatenate([jnp.full((1,), -1, docs.dtype), end_doc[:-1]])
-    carry_in = jnp.exp(cum) * (docb == last_doc[:, None]).astype(jnp.float32)[:, :, None]
-    tail = jnp.exp(cum[:, -1:] - cum) * (docb == end_doc[:, None]).astype(jnp.float32)[:, :, None] * dtb
-    tx = (tail[..., None] * xh.astype(jnp.float32)).astype(jnp.bfloat16)
-    fresh = jnp.einsum("bjhp,nbj->bhpn", tx, bb, preferred_element_type=jnp.float32)
-    states = [jnp.zeros((heads, HDIM, STATE), jnp.float32)]
-    for k in range(blocks - 1):
-        states.append(carry_in[k, -1][:, None, None] * states[-1] + fresh[k])
-    entering = jnp.stack(states).astype(jnp.bfloat16)
-    outer = jnp.einsum("nbi,bhpn->bihp", cb, entering, preferred_element_type=jnp.float32)
-    return (inner + outer * carry_in[..., None]).reshape(count, heads * HDIM)
+    )(
+        tokens, w_gate, w_xin, w_bc, w_dt.T, conv_x, conv_xb[None, :], conv_b, conv_bb[None, :],
+        bias, rate, skip, lengths,
+    )
 
 
 def shards(
@@ -614,55 +744,16 @@
 ):
     seqs = lax.axis_size("seq")
     tens = lax.axis_size("tensor")
-    here = lax.axis_index("seq")
-    own, depth = tokens.shape[0], w_gate.shape[0]
-    total = own * seqs * tens
-    chans = w_gate.shape[1] // seqs
-    heads = w_dt.shape[1] // seqs
-    parts = w_bc.shape[1] // (seqs * GROUPS)
-    small = jnp.concatenate(
-        [
-            w_bc.T.reshape(seqs, parts, GROUPS, depth)
-            .transpose(0, 2, 1, 3)
-            .reshape(seqs, parts * GROUPS, depth),
-            w_dt.T.reshape(seqs, heads, depth),
-            jnp.zeros((seqs, -(parts * GROUPS + heads) % 16, depth), jnp.bfloat16),
-        ],
-        axis=1,
-    )
-    gate, xin, small = project_in(tokens, w_gate, w_xin, small, seqs, tens // 2)
-    docs = doc_ids(lengths, jnp.arange(total, dtype=jnp.int32))
-
-    def mine(vector, width, axis=0):
-        return lax.dynamic_slice_in_dim(vector, here * width, width, axis)
-
-    xc = conv_full(xin, mine(conv_x, chans, 1), mine(conv_x_bias, chans), docs, 0)
-
-    def grouped(vector):
-        lead = vector.shape[:-1]
-        vector = mine(vector, parts * GROUPS, len(lead)).reshape(lead + (parts, GROUPS))
-        return jnp.swapaxes(vector, -1, -2).reshape(lead + (parts * GROUPS,))
-
-    bcc = conv_full(small[: parts * GROUPS], grouped(conv_bc), grouped(conv_bc_bias), docs, 1)
-    fold = 16 // parts
-    bcc = bcc.reshape(GROUPS, parts, fold, total // fold).transpose(0, 2, 1, 3)
-    bcc = to_groups(bcc.reshape(GROUPS, 16, total // fold), seqs)
-    bcc = bcc.reshape(seqs, tens, fold, parts, total // fold).transpose(1, 0, 3, 2, 4)
-    bcc = bcc.reshape(2 * STATE, total)
-    dtin = small[parts * GROUPS : parts * GROUPS + heads].T.astype(jnp.float32)
-    dtv = jax.nn.softplus(dtin + mine(dt_bias, heads)[None, :])
-    y = scan_heads(
-        xc, dtv, mine(decay_rate, heads), bcc[:STATE], bcc[STATE:], docs, min(STRETCH, total)
-    )
-    y = y + jnp.repeat(mine(d_skip, heads), HDIM)[None, :] * xc.astype(jnp.float32)
-    gated = (y * jax.nn.silu(gate.astype(jnp.float32))).astype(jnp.bfloat16)
-    return project_out(gated, norm_gain, w_out, own, seqs, tens // 2)
+    gated = mix_in(
+        tokens, w_gate, w_xin, w_bc, w_dt, conv_x, conv_x_bias, conv_bc, conv_bc_bias,
+        dt_bias, decay_rate, d_skip, lengths,
+    )
+    return project_out(gated, norm_gain, w_out, tokens.shape[0], seqs, tens // 2)
 
 
 def solution(mesh):
     seqs, tens = mesh.shape["seq"], mesh.shape["tensor"]
-    heads = INNER // HDIM
-    narrow = tens == GROUPS and heads % (seqs * tens) == 0 and 2 * STATE == 8 * seqs * tens
+    narrow = seqs == SEQS and tens == GROUPS == 2 * CHIPS
     body = shards if narrow else shards_wide
     in_specs = (
         P(("seq", "tensor"), None),

time: 173 us -> 136 us (0.79)
  Pallas kernels: 145 us -> 125 us
  other arithmetic: 6 us -> 0 us
  local copies, waits for them, and re-layouts: 14.5 us -> 8.85 us
  matrix products: 5.24 us -> 0 us
    pallas_call x2 -> x1, Pallas kernels: 97.9 us -> 73.8 us  [mix_in(): pl.pallas_call(mix_kernel, out_shape=jax.ShapeDtypeStruct((total, WIDE),...]
    reshape x10 -> x0, local copies, waits for them, and re-layouts: 5.99 us -> none  [the longest x2 3.98 us: scan_heads(): return (inner + outer * carry_in[..., None]).reshape(count, heads * HDIM)]
    unnamed x32 -> x27, local copies, waits for them, and re-layouts: 2.96 us -> 8.85 us
    dot_general x5 -> x0, matrix products: 5.24 us -> none  [the longest x1 2.93 us: scan_heads(): jnp.einsum('bhij,bjhp->bihp', mixing.astype(jnp.bfloat16), xh, preferred_...]
    pallas_call x1, Pallas kernels: 47.1 us -> 51.1 us  [project_out(): pl.pallas_call(out_kernel, out_shape=jax.ShapeDtypeStruct((own, cols * se...]
    convert_element_type x6 -> x0, other arithmetic: 3.69 us -> none  [the longest x1 1.74 us: shards(): gated = (y * jax.nn.silu(gate.astype(jnp.float32))).astype(jnp.bfloat16)]
    slice x13 -> x0, local copies, waits for them, and re-layouts: 2.31 us -> none  [the longest x3 1 us: conv_full(): summed = across(weights[CONV - 1]) * values + across(bias)]
    dynamic_slice x6 -> x0, local copies, waits for them, and re-layouts: 1.95 us -> none  [mine(): return lax.dynamic_slice_in_dim(vector, here * width, width, axis)]
where the time goes in v1:
time: 136 us; the launch traced here: 134 us
  Pallas kernels  125 us (92%)
  local copies, waits for them, and re-layouts  8.85 us (7%)
    pallas_call x1, Pallas kernels, mix_in(): pl.pallas_call(mix_kernel, out_shape=jax.ShapeDtypeStruct((total, WIDE),...  73.8 us
    pallas_call x1, Pallas kernels, project_out(): pl.pallas_call(out_kernel, out_shape=jax.ShapeDtypeStruct((own, cols * se...  51.1 us
    unnamed x27, local copies, waits for them, and re-layouts  8.85 us

profile of v1, /device:TPU:0, one launch (start us, length us, event | category | flops | bytes accessed | tf_op | source)
XLA Modules:
  0.0 133.9 jit_solution(366399720614587102)
XLA Ops:
  0.0 0.0 copy-start.1
  0.0 1.0 copy-done.1
  1.0 0.0 copy-start.2
  1.0 0.9 copy-done.2
  2.0 0.0 copy-start.3
  2.0 0.8 copy-done.3
  2.8 0.0 copy-start.4
  2.8 0.7 copy-done.4
  3.5 0.0 copy-start.6
  3.5 0.7 copy-done.6
  4.2 0.0 copy-start.7
  4.2 0.7 copy-done.7
  4.8 0.0 copy-start.8
  4.8 0.7 copy-done.8
  5.5 0.0 copy-start.9
  5.5 0.7 copy-done.9
  6.2 0.0 copy-start.10
  6.2 0.7 copy-done.10
  6.8 0.0 copy-start.11
  6.8 0.7 copy-done.11
  7.5 0.0 copy-start.12
  7.5 0.7 copy-done.12
  8.1 0.0 copy-start
  8.1 0.0 copy-start.5
  8.2 73.8 %shard_map.145.g_ref = bf16[1024,256]{1,0:T(8,128)(2,1)S(1)} custom-call(bf16[32,4096]{1,0:T(8,128)(2,1)S(1)} %copy-done.2, bf16[1024,1024]{1,0:T(8,128)(2,1)} %wg_hbm.1, bf16[1024,1024]{1,0:T(8,128)(2,1)} %wx_hbm.1, bf16[1024,256]{1,0:T(8,128)(2,1)S(1)} %copy-done.1, bf16[16,1024]{1,0:T(8,128)(2,1)S(1)} %bitcast.4, f32[4,1024]{1,0:T(4,128)S(1)} %copy-done.4, ...), custom_call_target="tpu_custom_call" | custom-call | tf_op jit(solution)/shard_map/pallas_call | solution.py:690
  82.0 0.0 copy-done
  82.0 0.0 copy-done.5
  82.0 51.1 %shard_map.146 = bf16[32,4096]{1,0:T(8,128)(2,1)S(1)} custom-call(bf16[1024,256]{1,0:T(8,128)(2,1)S(1)} %shard_map.145.g_ref, f32[1,1024]{1,0:T(1,128)S(1)} %bitcast.5, bf16[1024,1024]{1,0:T(8,128)(2,1)S(1)} %copy-done), custom_call_target="tpu_custom_call" | custom-call | tf_op jit(solution)/shard_map/pallas_call | solution.py:340
  133.2 0.7 copy.17
Async XLA Ops:
  0.0 1.0 copy-start.1
  1.0 0.9 copy-start.2
  2.0 0.8 copy-start.3
  2.8 0.7 copy-start.4
  3.5 0.7 copy-start.6
  4.2 0.7 copy-start.7
  4.8 0.7 copy-start.8
  5.5 0.7 copy-start.9
  6.2 0.7 copy-start.10
  6.8 0.7 copy-start.11
  7.5 0.7 copy-start.12
  8.1 73.8 %copy-start = (bf16[1024,1024]{1,0:T(8,128)(2,1)S(1)}, bf16[1024,1024]{1,0:T(8,128)(2,1)}, u32[]{:S(2)}) copy-start(bf16[1024,1024]{1,0:T(8,128)(2,1)} %w_ref.1) | copy-start | bytes 6291460
  8.1 73.9 %copy-start.5 = (f32[1024]{0:T(1024)S(1)}, f32[1024]{0:T(1024)}, u32[]{:S(2)}) copy-start(f32[1024]{0:T(1024)} %param.27) | copy-start | bytes 12292

commit v2 on v1

--- a/solution.py
+++ b/solution.py
@@ -222,146 +222,6 @@
     )
 
 
-def places():
-    s, t = lax.axis_index("seq"), lax.axis_index("tensor")
-    seqs, chips = lax.axis_size("seq"), lax.axis_size("tensor") // 2
-    z, c = t // 2, t % 2
-
-    def along(ds, dz):
-        return lax.rem(s + ds, seqs), lax.rem(z + dz, chips)
-
-    return s, z, c, seqs, chips, along
-
-
-def out_kernel(
-    g_ref, gain_ref, w_ref, out_ref, held, normed, part, sib, pair, got,
-    g_send, g_recv, p_send, p_recv, o_send, o_recv,
-):
-    s, z, c, seqs, chips, along = places()
-    span = g_ref.shape[0] // seqs
-    width = g_ref.shape[1]
-    own = out_ref.shape[0]
-    cols = w_ref.shape[1]
-    sibling = (s, 2 * z + 1 - c)
-    offsets = [(ds, dz) for ds in range(seqs) for dz in range(chips) if ds or dz]
-    enter([(along(ds, dz)[0], 2 * along(ds, dz)[1] + c) for ds, dz in offsets] + [sibling])
-    order = list(range(1, seqs)) + [0]
-    gathers = {}
-    for k in order:
-        for ds in range(1, seqs):
-            rows = pl.ds(pl.multiple_of(lax.rem(s + ds + k, seqs) * span, span), span)
-            gathers[k, ds] = remote(
-                g_ref.at[rows],
-                held.at[ds, rows],
-                g_send.at[k, ds],
-                g_recv.at[k, ds],
-                (along(ds, 0)[0], 2 * z + c),
-            )
-            gathers[k, ds].start()
-    pairs, sends = {}, []
-
-    def finish(k):
-        q = lax.rem(s + k, seqs)
-        pairs[k].wait_recv()
-        for dz in range(chips):
-            there = along(0, dz)[1]
-            both = part[q, there, c].astype(jnp.float32) + sib[q, there].astype(jnp.float32)
-            if k == 0 and dz == 0:
-                got[0, 0] = both.astype(jnp.bfloat16)
-            else:
-                pair[k, dz] = both.astype(jnp.bfloat16)
-                sends.append(
-                    remote(
-                        pair.at[k, dz],
-                        got.at[k, dz],
-                        o_send.at[k, dz],
-                        o_recv.at[k, dz],
-                        (q, 2 * there + c),
-                    )
-                )
-                sends[-1].start()
-
-    for step, k in enumerate(order):
-        q = lax.rem(s + k, seqs)
-        rows = pl.ds(pl.multiple_of(q * span, span), span)
-        for ds in range(1, seqs):
-            gathers[k, ds].wait_recv()
-        blocks = [g_ref[rows, :].astype(jnp.float32)] + [
-            held[ds, rows, :].astype(jnp.float32) for ds in range(1, seqs)
-        ]
-        squares = blocks[0] * blocks[0]
-        for b in blocks[1:]:
-            squares = squares + b * b
-        scale = lax.rsqrt(jnp.sum(squares, axis=1, keepdims=True) / (width * seqs) + 1e-05)
-        froms = [pl.multiple_of(lax.rem(s + seqs - ds, seqs) * width, width) for ds in range(seqs)]
-        for ds in range(seqs):
-            normed[ds] = (blocks[ds] * scale * gain_ref[:, pl.ds(froms[ds], width)]).astype(
-                jnp.bfloat16
-            )
-        tile = 256
-
-        def column(n, _):
-            here = pl.ds(pl.multiple_of(n * tile, tile), tile)
-            acc = jnp.zeros((span, tile), jnp.float32)
-            for ds in range(seqs):
-                acc = acc + jnp.dot(
-                    normed[ds],
-                    w_ref[pl.ds(froms[ds], width), here],
-                    preferred_element_type=jnp.float32,
-                )
-            part[q, :, :, :, here] = acc.astype(jnp.bfloat16).reshape(chips, 2, own, tile)
-            return 0
-
-        lax.fori_loop(0, cols // tile, column, 0)
-        pairs[k] = remote(
-            part.at[q, :, 1 - c], sib.at[q], p_send.at[k], p_recv.at[k], sibling
-        )
-        pairs[k].start()
-        if step:
-            finish(order[step - 1])
-    finish(order[-1])
-    for copy in sends:
-        copy.wait_recv()
-    for ds in range(seqs):
-        total = got[ds, 0].astype(jnp.float32)
-        for dz in range(1, chips):
-            total = total + got[ds, dz].astype(jnp.float32)
-        begin = pl.multiple_of(lax.rem(s + seqs - ds, seqs) * cols, cols)
-        out_ref[:, pl.ds(begin, cols)] = total.astype(jnp.bfloat16)
-    for copy in list(gathers.values()) + list(pairs.values()) + sends:
-        copy.wait_send()
-
-
-def project_out(gated, gain, w_out, own, seqs, chips):
-    total, width = gated.shape
-    cols = w_out.shape[1]
-    dma = pltpu.SemaphoreType.DMA
-    vmem = pl.BlockSpec(memory_space=pltpu.VMEM)
-    return pl.pallas_call(
-        out_kernel,
-        out_shape=jax.ShapeDtypeStruct((own, cols * seqs), jnp.bfloat16),
-        in_specs=[vmem] * 3,
-        out_specs=vmem,
-        scratch_shapes=[
-            pltpu.VMEM((seqs, total, width), jnp.bfloat16),
-            pltpu.VMEM((seqs, total // seqs, width), jnp.bfloat16),
-            pltpu.VMEM((seqs, chips, 2, own, cols), jnp.bfloat16),
-            pltpu.VMEM((seqs, chips, own, cols), jnp.bfloat16),
-            pltpu.VMEM((seqs, chips, own, cols), jnp.bfloat16),
-            pltpu.VMEM((seqs, chips, own, cols), jnp.bfloat16),
-            dma((seqs, seqs)),
-            dma((seqs, seqs)),
-            dma((seqs,)),
-            dma((seqs,)),
-            dma((seqs, chips)),
-            dma((seqs, chips)),
-        ],
-        compiler_params=pltpu.CompilerParams(
-            collective_id=1, has_side_effects=True, vmem_limit_bytes=40 * 2**20
-        ),
-    )(gated, gain[None, :], w_out)
-
-
 SEQS, CHIPS, OWN, SPAN, WIDE, HALF = 4, 4, 32, 256, 256, 128
 LOG2E = 1.4426950408889634
 
@@ -424,9 +284,11 @@
 
 
 def mix_kernel(
-    tok_ref, wg_hbm, wx_hbm, wb_hbm, wdt_ref, cx_ref, cxb_ref, cb_ref, cbb_ref,
-    bias_s, rate_s, skip_s, len_s, out_ref,
-    tok, wg, wx, wb, rel, xs, xc, bs, halo, bct, bca, bcp, dts, dtg, dtv,
+    tok_hbm, wg_hbm, wx_hbm, wb_hbm, wdt_hbm, cx_hbm, cxb_hbm, cb_hbm, cbb_hbm, gain_hbm, wo_hbm,
+    bias_hbm, rate_hbm, skip_hbm, len_hbm, out_ref,
+    wg, wx, wb, wdt, cx, cxb, cb, cbb, gain, wo, bias_s, rate_s, skip_s, len_s,
+    tok, rel, xs, xc, bs, halo, bct, bca, bcp, dts, dtg, dtv,
+    held, normed, part, sib, pair, got, done, res,
     *rest,
 ):
     big, rest = rest[:11], rest[11:]
@@ -435,14 +297,21 @@
         w_sem, t_send, t_recv, zu_send, zd_send, z_recv, f_send, f_recv,
         g_send, g_recv, b_send, b_recv, h_send, h_recv, d_send, d_recv,
         e_send, e_recv, a_send, a_recv,
+        y_send, y_recv, p_send, p_recv, r_send, r_recv, o_send, o_recv,
     ) = rest
     s, t = lax.axis_index("seq"), lax.axis_index("tensor")
     tens = 2 * CHIPS
     z, c = t // 2, t % 2
     sibling = (s, 2 * z + 1 - c)
+    depth = wx.shape[0]
+    own_cols = pl.ds(pl.multiple_of(s * depth, depth), depth)
     loads = [
         pltpu.make_async_copy(src, dst, w_sem.at[i])
-        for i, (src, dst) in enumerate(((wb_hbm, wb), (wx_hbm, wx), (wg_hbm, wg)))
+        for i, (src, dst) in enumerate((
+            (len_hbm, len_s), (tok_hbm.at[:, own_cols], tok.at[z, c, s]), (wb_hbm, wb), (wx_hbm, wx),
+            (wdt_hbm, wdt), (wg_hbm, wg), (cb_hbm, cb), (cbb_hbm, cbb), (cx_hbm, cx), (cxb_hbm, cxb),
+            (bias_hbm, bias_s), (rate_hbm, rate_s), (skip_hbm, skip_s), (gain_hbm, gain), (wo_hbm, wo),
+        ))
     ]
     for load in loads:
         load.start()
@@ -450,17 +319,16 @@
     across = [(s, lax.rem(t + d, tens)) for d in range(1, tens)]
     enter(along + across)
 
-    depth = wx.shape[0]
     spread = [
         remote(
-            tok_ref.at[:, pl.ds(pl.multiple_of(peer[0] * depth, depth), depth)],
+            tok_hbm.at[:, pl.ds(pl.multiple_of(peer[0] * depth, depth), depth)],
             tok.at[z, c, s], t_send.at[i], t_recv.at[i], peer,
         )
         for i, peer in enumerate(along)
     ]
     for copy in spread:
         copy.start()
-    tok[z, c, s] = tok_ref[:, pl.ds(pl.multiple_of(s * depth, depth), depth)]
+    loads[0].wait()
 
     total = SEQS * SPAN
     pos = lax.broadcasted_iota(jnp.int32, (total, HALF), 0)
@@ -487,6 +355,7 @@
         if i:
             up.wait_recv()
         else:
+            loads[1].wait()
             for copy in spread:
                 copy.wait_recv()
         pl.when(goes_up)(up.start)
@@ -508,11 +377,11 @@
         arrive(i)
         rows = tok[order[i]].reshape(SPAN, depth)
         if i == 0:
-            loads[0].wait()
+            loads[2].wait()
         bcp[...] = jnp.dot(rows, wb[...], preferred_element_type=jnp.float32).reshape(2, SEQS, OWN, WIDE)
         sumb.emit(i, lambda r: bcp[:, s ^ r].reshape(2 * OWN, WIDE))
         if i == 0:
-            loads[1].wait()
+            loads[3].wait()
         sums.emit(i, product(rows, wx))
         if i:
             sumb.relay(i - 1)
@@ -522,9 +391,10 @@
     def span_rows(q):
         return tok[:, :, q].reshape(SPAN, depth)
 
+    loads[4].wait()
     for q in range(SEQS):
         dts[:, q * SPAN : (q + 1) * SPAN] = lax.dot_general(
-            wdt_ref[...], span_rows(q), (((1,), (1,)), ((), ())), preferred_element_type=jnp.float32
+            wdt[...], span_rows(q), (((1,), (1,)), ((), ())), preferred_element_type=jnp.float32
         ).astype(jnp.bfloat16)
     steps = [
         remote(dts, dtg.at[i], d_send.at[i], d_recv.at[i], peer) for i, peer in enumerate(along)
@@ -537,9 +407,11 @@
     edge = remote(halo.at[0], halo.at[1], h_send, h_recv, (lax.rem(s + 1, SEQS), t))
     edge.start()
     sums.relay(CHIPS - 1)
-    loads[2].wait()
+    loads[5].wait()
     sums.emit(4, product(span_rows(0), wg))
 
+    for load in loads[6:]:
+        load.wait()
     edge.wait_recv()
     bs[:16, :] = halo[1].astype(jnp.float32)
     away = rel[pl.ds(pl.multiple_of(s * SPAN, SPAN), SPAN), :1]
@@ -551,7 +423,7 @@
             out = out + jnp.where(away >= back, tap, 0.0)
         return silu(out).astype(jnp.bfloat16)
 
-    bcc = conv(bs, 16, cb_ref[...], cbb_ref[...], away)
+    bcc = conv(bs, 16, cb[...], cbb[...], away)
     to = lax.broadcasted_iota(jnp.int32, (WIDE, WIDE), 0)
     frm = lax.broadcasted_iota(jnp.int32, (WIDE, WIDE), 1)
     pick = (frm == (to % 32) * GROUPS + to // 32).astype(jnp.float32).astype(jnp.bfloat16)
@@ -589,7 +461,7 @@
     mine = pl.ds(pl.multiple_of(s * WIDE, WIDE), WIDE)
     for q in range(SEQS):
         xc[q * SPAN : (q + 1) * SPAN, :] = conv(
-            xs, 16 + q * SPAN, cx_ref[:, mine], cxb_ref[:, mine], rel[q * SPAN : (q + 1) * SPAN, :1]
+            xs, 16 + q * SPAN, cx[:, mine], cxb[:, mine], rel[q * SPAN : (q + 1) * SPAN, :1]
         ).astype(jnp.float32)
     sums.relay(5)
     for copy in steps:
@@ -617,6 +489,67 @@
         skip = jnp.where(lane[:1] == h, skip_s[heads * s + h], skip)
     for copy in groups:
         copy.wait_recv()
+
+    cols_out = wo.shape[1]
+    gathers = [
+        [
+            remote(held.at[s, q], held.at[s, q], y_send.at[q, i], y_recv.at[q, i], peer)
+            for i, peer in enumerate(along)
+        ]
+        for q in range(SEQS)
+    ]
+    pairs = [
+        remote(part.at[q, 1 - c], sib.at[q], p_send.at[q], p_recv.at[q], sibling) for q in range(SEQS)
+    ]
+
+    def reduces(q):
+        peers = [lax.rem(z + d, CHIPS) for d in range(1, CHIPS)]
+        return [
+            remote(pair.at[q, to], got.at[q, i], r_send.at[q, i], r_recv.at[q, i], (s, 2 * to + c))
+            for i, to in enumerate(peers)
+        ]
+
+    def deliver(q, frm):
+        return remote(done.at[q], res.at[frm], o_send.at[q], o_recv.at[frm], (q, t))
+
+    def project(q):
+        for copy in gathers[q]:
+            copy.wait_recv()
+        squares = jnp.zeros((SPAN, WIDE), jnp.float32)
+        for k in range(SEQS):
+            piece = held[k, q].astype(jnp.float32)
+            squares = squares + piece * piece
+        scale = lax.rsqrt(jnp.sum(squares, axis=1, keepdims=True) / (SEQS * WIDE) + 1e-05)
+        for k in range(SEQS):
+            wide = slice(k * WIDE, (k + 1) * WIDE)
+            normed[:, wide] = (held[k, q].astype(jnp.float32) * scale * gain[:, wide]).astype(jnp.bfloat16)
+        for n in range(cols_out // WIDE):
+            wide = slice(n * WIDE, (n + 1) * WIDE)
+            acc = jnp.dot(normed[...], wo[:, wide], preferred_element_type=jnp.float32)
+            acc = acc.astype(jnp.bfloat16).reshape(CHIPS, 2, OWN, WIDE)
+            for half in range(2):
+                part[q, half, :, :, wide] = acc[:, half]
+        pairs[q].start()
+
+    def combine(q):
+        pairs[q].wait_recv()
+        pair[q] = (part[q, c].astype(jnp.float32) + sib[q].astype(jnp.float32)).astype(jnp.bfloat16)
+        for copy in reduces(q):
+            copy.start()
+
+    def collect(q):
+        for copy in reduces(q):
+            copy.wait_recv()
+        total = pair[q, z].astype(jnp.float32)
+        for i in range(CHIPS - 1):
+            total = total + got[q, i].astype(jnp.float32)
+        done[q] = total.astype(jnp.bfloat16)
+        pl.when(s != q)(deliver(q, s).start)
+
+        @pl.when(s == q)
+        def _():
+            res[q] = done[q]
+
     state = jnp.zeros((STATE, WIDE), jnp.float32)
     local = to[:, :1]
     for q in range(SEQS):
@@ -660,7 +593,23 @@
         if q == 1:
             sums.relay(7)
         gate = sums.final(4 + q).astype(jnp.float32)
-        out_ref[here, :] = (y * silu(gate)).astype(jnp.bfloat16)
+        held[s, q] = (y * silu(gate)).astype(jnp.bfloat16)
+        for copy in gathers[q]:
+            copy.start()
+        if q:
+            project(q - 1)
+        if q > 1:
+            combine(q - 2)
+    project(SEQS - 1)
+    combine(SEQS - 2)
+    collect(0)
+    collect(SEQS - 3)
+    combine(SEQS - 1)
+    collect(SEQS - 2)
+    collect(SEQS - 1)
+    for q in range(SEQS):
+        pl.when(s != q)(deliver(0, q).wait_recv)
+        out_ref[:, q * cols_out : (q + 1) * cols_out] = res[q]
 
     for zb in range(CHIPS):
         up, down, over, goes_up, goes_down = hops(zb)
@@ -669,17 +618,22 @@
         over.wait_send()
     for copy in spread + steps + [edge] + swaps + groups:
         copy.wait_send()
+    for q in range(SEQS):
+        for copy in gathers[q] + [pairs[q]] + reduces(q):
+            copy.wait_send()
+        pl.when(s != q)(deliver(q, s).wait_send)
     for u in range(8):
         sums.drain(u)
     for u in range(4):
         sumb.drain(u)
 
 
-def mix_in(tokens, w_gate, w_xin, w_bc, w_dt, conv_x, conv_xb, conv_b, conv_bb, bias, rate, skip, lengths):
-    depth, width = w_xin.shape
+def mix(operands, own, seqs):
+    tokens, w_gate, w_xin, w_bc, w_dt, conv_x, conv_xb, conv_b, conv_bb, gain, w_out = operands[:11]
+    depth = w_xin.shape[0]
     total = SEQS * SPAN
+    cols = w_out.shape[1]
     dma = pltpu.SemaphoreType.DMA
-    vmem, smem, anyw = (pl.BlockSpec(memory_space=m) for m in (pltpu.VMEM, pltpu.SMEM, pl.ANY))
     bf, f32 = jnp.bfloat16, jnp.float32
 
     def sums(n, rows):
@@ -689,14 +643,13 @@
 
     return pl.pallas_call(
         mix_kernel,
-        out_shape=jax.ShapeDtypeStruct((total, WIDE), bf),
-        in_specs=[vmem, anyw, anyw, anyw] + [vmem] * 5 + [smem] * 4,
-        out_specs=vmem,
-        scratch_shapes=[
+        out_shape=jax.ShapeDtypeStruct((own, cols * seqs), bf),
+        in_specs=[pl.BlockSpec(memory_space=pl.ANY)] * len(operands),
+        out_specs=pl.BlockSpec(memory_space=pltpu.VMEM),
+        scratch_shapes=[pltpu.VMEM(a.shape, a.dtype) for a in operands[1:11]]
+        + [pltpu.SMEM(a.shape, a.dtype) for a in operands[11:]]
+        + [
             pltpu.VMEM((CHIPS, 2, SEQS, OWN, depth), bf),
-            pltpu.VMEM(w_gate.shape, bf),
-            pltpu.VMEM(w_xin.shape, bf),
-            pltpu.VMEM(w_bc.shape, bf),
             pltpu.VMEM((total, HALF), jnp.int32),
             pltpu.VMEM((16 + total, WIDE), f32),
             pltpu.VMEM((total, WIDE), f32),
@@ -708,21 +661,27 @@
             pltpu.VMEM((16, total), bf),
             pltpu.VMEM((3, 16, total), bf),
             pltpu.VMEM((16, total), f32),
+            pltpu.VMEM((SEQS, SEQS, SPAN, WIDE), bf),
+            pltpu.VMEM((SPAN, SEQS * WIDE), bf),
+            pltpu.VMEM((SEQS, 2, CHIPS, OWN, cols), bf),
+            pltpu.VMEM((SEQS, CHIPS, OWN, cols), bf),
+            pltpu.VMEM((SEQS, CHIPS, OWN, cols), bf),
+            pltpu.VMEM((SEQS, CHIPS - 1, OWN, cols), bf),
+            pltpu.VMEM((SEQS, OWN, cols), bf),
+            pltpu.VMEM((SEQS, OWN, cols), bf),
         ]
         + sums(8, SPAN)
         + sums(4, 2 * OWN)
         + [
-            dma((3,)), dma((3,)), dma((3,)), dma((4,)), dma((4,)), dma((4,)), dma((4,)), dma((4,)),
+            dma((15,)), dma((3,)), dma((3,)), dma((4,)), dma((4,)), dma((4,)), dma((4,)), dma((4,)),
             dma((8, 4)), dma((8, 4)), dma((4, 4)), dma((4, 4)),
             dma, dma, dma((3,)), dma((3,)), dma((7,)), dma((7,)), dma((3,)), dma((3,)),
+            dma((4, 3)), dma((4, 3)), dma((4,)), dma((4,)), dma((4, 3)), dma((4, 3)), dma((4,)), dma((4,)),
         ],
         compiler_params=pltpu.CompilerParams(
-            collective_id=2, has_side_effects=True, vmem_limit_bytes=52 * 2**20
+            collective_id=2, has_side_effects=True, vmem_limit_bytes=56 * 2**20
         ),
-    )(
-        tokens, w_gate, w_xin, w_bc, w_dt.T, conv_x, conv_xb[None, :], conv_b, conv_bb[None, :],
-        bias, rate, skip, lengths,
-    )
+    )(*operands)
 
 
 def shards(
@@ -742,13 +701,11 @@
     w_out,
     lengths,
 ):
-    seqs = lax.axis_size("seq")
-    tens = lax.axis_size("tensor")
-    gated = mix_in(
-        tokens, w_gate, w_xin, w_bc, w_dt, conv_x, conv_x_bias, conv_bc, conv_bc_bias,
-        dt_bias, decay_rate, d_skip, lengths,
-    )
-    return project_out(gated, norm_gain, w_out, tokens.shape[0], seqs, tens // 2)
+    operands = (
+        tokens, w_gate, w_xin, w_bc, w_dt.T, conv_x, conv_x_bias[None, :], conv_bc, conv_bc_bias[None, :],
+        norm_gain[None, :], w_out, dt_bias, decay_rate, d_skip, lengths,
+    )
+    return mix(operands, tokens.shape[0], lax.axis_size("seq"))
 
 
 def solution(mesh):

time: 136 us -> 117 us (0.86); the launches traced: 134 us -> 117 us
  Pallas kernels: 125 us -> 115 us
  local copies, waits for them, and re-layouts: 8.85 us -> 1.67 us
    pallas_call x2 -> x1, Pallas kernels: 125 us -> 115 us  [mix(): pl.pallas_call(mix_kernel, out_shape=jax.ShapeDtypeStruct((own, cols * se...]
    unnamed x27 -> x1, local copies, waits for them, and re-layouts: 8.85 us -> 1.67 us
where the time goes in v2:
time: 117 us
  Pallas kernels  115 us (98%)
  local copies, waits for them, and re-layouts  1.67 us (1%)
    pallas_call x1, Pallas kernels, mix(): pl.pallas_call(mix_kernel, out_shape=jax.ShapeDtypeStruct((own, cols * se...  115 us

profile of v2, /device:TPU:0, one launch (start us, length us, event | category | flops | bytes accessed | tf_op | source)
XLA Modules:
  0.0 117.1 jit_solution(1103107892543435979)
XLA Ops:
  0.0 115.4 %shard_map.145 = bf16[32,4096]{1,0:T(8,128)(2,1)} custom-call(bf16[32,4096]{1,0:T(8,128)(2,1)} %tok_hbm.1, bf16[1024,1024]{1,0:T(8,128)(2,1)} %wg_hbm.1, bf16[1024,1024]{1,0:T(8,128)(2,1)} %wx_hbm.1, bf16[1024,256]{1,0:T(8,128)(2,1)} %wb_hbm.1, bf16[16,1024]{1,0:T(8,128)(2,1)} %bitcast.4, f32[4,1024]{1,0:T(4,128)} %cx_hbm.1, f32[1,1024]{1,0:T(1,128)} %bitcast.5, ...), custom_call_target="tpu_custom_call" | custom-call | tf_op jit(solution)/shard_map/pallas_call | solution.py:644
  115.4 1.7 %copy.17 = bf16[32,4096]{1,0:T(8,128)(2,1)} copy(bf16[32,4096]{1,0:T(8,128)(2,1)} %shard_map.145) | data formatting | bytes 524288

commit v3 on v2

--- a/solution.py
+++ b/solution.py
@@ -293,6 +293,7 @@
 ):
     big, rest = rest[:11], rest[11:]
     few, rest = rest[:11], rest[11:]
+    rim, rest = rest[:11], rest[11:]
     (
         w_sem, t_send, t_recv, zu_send, zd_send, z_recv, f_send, f_recv,
         g_send, g_recv, b_send, b_recv, h_send, h_recv, d_send, d_recv,
@@ -342,29 +343,37 @@
     last = 3 * (1 - z // 2)
     order = [z, first, 6 - z - first - last, last]
 
-    def hops(zb):
-        part = tok.at[zb, c]
-        up = remote(part, part, zu_send.at[zb], z_recv.at[zb], (s, 2 * lax.rem(z + 1, CHIPS) + c))
-        down = remote(part, part, zd_send.at[zb], z_recv.at[zb], (s, 2 * lax.rem(z + CHIPS - 1, CHIPS) + c))
-        over = remote(part, part, f_send.at[zb], f_recv.at[zb], sibling)
+    inner_chip = (z > 0) & (z < CHIPS - 1)
+
+    def hops(zb, r):
+        part = tok.at[zb, c, s ^ r]
+        up = remote(part, part, zu_send.at[zb, r], z_recv.at[zb, r], (s, 2 * lax.rem(z + 1, CHIPS) + c))
+        down = remote(
+            part, part, zd_send.at[zb, r], z_recv.at[zb, r], (s, 2 * lax.rem(z + CHIPS - 1, CHIPS) + c)
+        )
+        over = remote(part, part, f_send.at[zb, r], f_recv.at[zb, r], sibling)
         return up, down, over, (z < CHIPS - 1) & (zb <= z), (z > 0) & (zb >= z)
 
-    def arrive(i):
-        zb = order[i]
-        up, down, over, goes_up, goes_down = hops(zb)
-        if i:
-            up.wait_recv()
-        else:
-            loads[1].wait()
-            for copy in spread:
-                copy.wait_recv()
-        pl.when(goes_up)(up.start)
-        pl.when(goes_down)(down.start)
-        over.start()
-        over.wait_recv()
+    def arrive(i, pieces=range(1, SEQS)):
+        for r in pieces:
+            up, down, over, goes_up, goes_down = hops(order[i], r)
+            if i:
+                up.wait_recv()
+            elif r:
+                spread[r - 1].wait_recv()
+            else:
+                loads[1].wait()
+            pl.when(goes_up)(up.start)
+            pl.when(goes_down)(down.start)
+            over.start()
+
+    def arrive_if(which, i, pieces=range(SEQS)):
+        if i < CHIPS:
+            pl.when(which)(lambda: arrive(i, pieces))
 
     sums = Sums(big, (g_send, g_recv), s, z, c)
     sumb = Sums(few, (b_send, b_recv), s, z, c)
+    sumh = Sums(rim, (h_send, h_recv), s, z, c)
 
     def product(rows, w):
         def get(r):
@@ -373,13 +382,31 @@
 
         return get
 
+    arrive(0, [0])
+    arrive(1, [0])
+    arrive_if(inner_chip, 2, [0])
+    arrive(0)
     for i in range(CHIPS):
-        arrive(i)
+        if i:
+            if i == 1:
+                arrive(i)
+            else:
+                arrive_if(~inner_chip, i)
+            arrive_if(inner_chip, i + 1, range(1 if i == 1 else 0, SEQS))
+        for r in range(SEQS):
+            hops(order[i], r)[2].wait_recv()
         rows = tok[order[i]].reshape(SPAN, depth)
         if i == 0:
             loads[2].wait()
         bcp[...] = jnp.dot(rows, wb[...], preferred_element_type=jnp.float32).reshape(2, SEQS, OWN, WIDE)
         sumb.emit(i, lambda r: bcp[:, s ^ r].reshape(2 * OWN, WIDE))
+
+        @pl.when(order[i] == CHIPS - 1)
+        def _():
+            halo[...] = bcp[1, :, OWN - 16 :, :]
+
+        if i == CHIPS - 1:
+            sumh.emit(0, lambda r: halo[lax.rem((s ^ r) + SEQS - 1, SEQS)])
         if i == 0:
             loads[3].wait()
         sums.emit(i, product(rows, wx))
@@ -387,11 +414,45 @@
             sumb.relay(i - 1)
             sums.relay(i - 1)
     sumb.relay(CHIPS - 1)
+    sumh.relay(0)
 
     def span_rows(q):
         return tok[:, :, q].reshape(SPAN, depth)
 
-    loads[4].wait()
+    loads[5].wait()
+    sums.emit(4, product(span_rows(0), wg))
+    bs[:16, :] = sumh.final(0).astype(jnp.float32)
+    for i in range(CHIPS):
+        bs[pl.ds(pl.multiple_of(16 + order[i] * 2 * OWN, 16), 2 * OWN), :] = sumb.final(i).astype(jnp.float32)
+
+    for load in loads[4:5] + loads[6:]:
+        load.wait()
+    away = rel[pl.ds(pl.multiple_of(s * SPAN, SPAN), SPAN), :1]
+
+    def conv(src, begin, w, bias, away):
+        out = w[CONV - 1 :, :] * src[begin : begin + SPAN, :] + bias
+        for back in range(1, CONV):
+            tap = w[CONV - 1 - back : CONV - back, :] * src[begin - back : begin - back + SPAN, :]
+            out = out + jnp.where(away >= back, tap, 0.0)
+        return silu(out).astype(jnp.bfloat16)
+
+    bcc = conv(bs, 16, cb[...], cbb[...], away)
+    to = lax.broadcasted_iota(jnp.int32, (WIDE, WIDE), 0)
+    frm = lax.broadcasted_iota(jnp.int32, (WIDE, WIDE), 1)
+    pick = (frm == (to % 32) * GROUPS + to // 32).astype(jnp.float32).astype(jnp.bfloat16)
+    bct[...] = (
+        lax.dot_general(pick, bcc, (((1,), (1,)), ((), ())), preferred_element_type=jnp.float32)
+        .astype(jnp.bfloat16)
+        .reshape(GROUPS, 32, SPAN)
+    )
+    swaps = [
+        remote(bct.at[peer[1]], bca.at[s, t], e_send.at[i], e_recv.at[i], peer)
+        for i, peer in enumerate(across)
+    ]
+    for copy in swaps:
+        copy.start()
+    bca[s, t] = bct[t]
+    sums.relay(CHIPS - 1)
     for q in range(SEQS):
         dts[:, q * SPAN : (q + 1) * SPAN] = lax.dot_general(
             wdt[...], span_rows(q), (((1,), (1,)), ((), ())), preferred_element_type=jnp.float32
@@ -401,50 +462,7 @@
     ]
     for copy in steps:
         copy.start()
-    for i in range(CHIPS):
-        bs[pl.ds(pl.multiple_of(16 + order[i] * 2 * OWN, 16), 2 * OWN), :] = sumb.final(i).astype(jnp.float32)
-    halo[0] = bs[16 + SPAN - 16 :, :].astype(jnp.bfloat16)
-    edge = remote(halo.at[0], halo.at[1], h_send, h_recv, (lax.rem(s + 1, SEQS), t))
-    edge.start()
-    sums.relay(CHIPS - 1)
-    loads[5].wait()
-    sums.emit(4, product(span_rows(0), wg))
-
-    for load in loads[6:]:
-        load.wait()
-    edge.wait_recv()
-    bs[:16, :] = halo[1].astype(jnp.float32)
-    away = rel[pl.ds(pl.multiple_of(s * SPAN, SPAN), SPAN), :1]
-
-    def conv(src, begin, w, bias, away):
-        out = w[CONV - 1 :, :] * src[begin : begin + SPAN, :] + bias
-        for back in range(1, CONV):
-            tap = w[CONV - 1 - back : CONV - back, :] * src[begin - back : begin - back + SPAN, :]
-            out = out + jnp.where(away >= back, tap, 0.0)
-        return silu(out).astype(jnp.bfloat16)
-
-    bcc = conv(bs, 16, cb[...], cbb[...], away)
-    to = lax.broadcasted_iota(jnp.int32, (WIDE, WIDE), 0)
-    frm = lax.broadcasted_iota(jnp.int32, (WIDE, WIDE), 1)
-    pick = (frm == (to % 32) * GROUPS + to // 32).astype(jnp.float32).astype(jnp.bfloat16)
-    bct[...] = (
-        lax.dot_general(pick, bcc, (((1,), (1,)), ((), ())), preferred_element_type=jnp.float32)
-        .astype(jnp.bfloat16)
-        .reshape(GROUPS, 32, SPAN)
-    )
-    swaps = [
-        remote(bct.at[peer[1]], bca.at[s, t], e_send.at[i], e_recv.at[i], peer)
-        for i, peer in enumerate(across)
-    ]
-    for copy in swaps:
-        copy.start()
-    bca[s, t] = bct[t]
-    for i in range(CHIPS):
-        full = sums.final(i).astype(jnp.float32).reshape(2, SEQS, OWN, WIDE)
-        for half in range(2):
-            for q in range(SEQS):
-                at = 16 + q * SPAN + half * OWN + order[i] * 2 * OWN
-                xs[pl.ds(pl.multiple_of(at, 16), OWN), :] = full[half, q]
+    sums.emit(5, product(span_rows(1), wg))
     for copy in swaps:
         copy.wait_recv()
     groups = [
@@ -453,10 +471,14 @@
     ]
     for copy in groups:
         copy.start()
-    sums.emit(5, product(span_rows(1), wg))
     sums.relay(4)
+    for i in range(CHIPS):
+        full = sums.final(i).astype(jnp.float32).reshape(2, SEQS, OWN, WIDE)
+        for half in range(2):
+            for q in range(SEQS):
+                at = 16 + q * SPAN + half * OWN + order[i] * 2 * OWN
+                xs[pl.ds(pl.multiple_of(at, 16), OWN), :] = full[half, q]
     sums.emit(6, product(span_rows(2), wg))
-    sums.emit(7, product(span_rows(3), wg))
     xs[:16, :] = jnp.zeros((16, WIDE), jnp.float32)
     mine = pl.ds(pl.multiple_of(s * WIDE, WIDE), WIDE)
     for q in range(SEQS):
@@ -464,6 +486,7 @@
             xs, 16 + q * SPAN, cx[:, mine], cxb[:, mine], rel[q * SPAN : (q + 1) * SPAN, :1]
         ).astype(jnp.float32)
     sums.relay(5)
+    sums.emit(7, product(span_rows(3), wg))
     for copy in steps:
         copy.wait_recv()
     dtv[...] = (
@@ -491,64 +514,73 @@
         copy.wait_recv()
 
     cols_out = wo.shape[1]
+    few_rows = OWN // 2
     gathers = [
         [
-            remote(held.at[s, q], held.at[s, q], y_send.at[q, i], y_recv.at[q, i], peer)
+            remote(held.at[s, k], held.at[s, k], y_send.at[k, i], y_recv.at[k, i], peer)
             for i, peer in enumerate(along)
         ]
-        for q in range(SEQS)
+        for k in range(2 * SEQS)
     ]
     pairs = [
-        remote(part.at[q, 1 - c], sib.at[q], p_send.at[q], p_recv.at[q], sibling) for q in range(SEQS)
+        remote(part.at[k, 1 - c], sib.at[k], p_send.at[k], p_recv.at[k], sibling)
+        for k in range(2 * SEQS)
     ]
 
-    def reduces(q):
+    def reduces(k):
         peers = [lax.rem(z + d, CHIPS) for d in range(1, CHIPS)]
         return [
-            remote(pair.at[q, to], got.at[q, i], r_send.at[q, i], r_recv.at[q, i], (s, 2 * to + c))
+            remote(pair.at[k, to], got.at[k, i], r_send.at[k, i], r_recv.at[k, i], (s, 2 * to + c))
             for i, to in enumerate(peers)
         ]
 
-    def deliver(q, frm):
-        return remote(done.at[q], res.at[frm], o_send.at[q], o_recv.at[frm], (q, t))
-
-    def project(q):
-        for copy in gathers[q]:
+    def deliver(k, frm):
+        return remote(done.at[k], res.at[frm, k % 2], o_send.at[k], o_recv.at[frm, k % 2], (k // 2, t))
+
+    def project(k):
+        for copy in gathers[k]:
             copy.wait_recv()
-        squares = jnp.zeros((SPAN, WIDE), jnp.float32)
-        for k in range(SEQS):
-            piece = held[k, q].astype(jnp.float32)
+        squares = jnp.zeros((SPAN // 2, WIDE), jnp.float32)
+        for n in range(SEQS):
+            piece = held[n, k].astype(jnp.float32)
             squares = squares + piece * piece
         scale = lax.rsqrt(jnp.sum(squares, axis=1, keepdims=True) / (SEQS * WIDE) + 1e-05)
-        for k in range(SEQS):
-            wide = slice(k * WIDE, (k + 1) * WIDE)
-            normed[:, wide] = (held[k, q].astype(jnp.float32) * scale * gain[:, wide]).astype(jnp.bfloat16)
+        for n in range(SEQS):
+            wide = slice(n * WIDE, (n + 1) * WIDE)
+            normed[:, wide] = (held[n, k].astype(jnp.float32) * scale * gain[:, wide]).astype(jnp.bfloat16)
         for n in range(cols_out // WIDE):
             wide = slice(n * WIDE, (n + 1) * WIDE)
             acc = jnp.dot(normed[...], wo[:, wide], preferred_element_type=jnp.float32)
-            acc = acc.astype(jnp.bfloat16).reshape(CHIPS, 2, OWN, WIDE)
+            acc = acc.reshape(CHIPS, 2, few_rows, WIDE).astype(jnp.bfloat16)
             for half in range(2):
-                part[q, half, :, :, wide] = acc[:, half]
-        pairs[q].start()
-
-    def combine(q):
-        pairs[q].wait_recv()
-        pair[q] = (part[q, c].astype(jnp.float32) + sib[q].astype(jnp.float32)).astype(jnp.bfloat16)
-        for copy in reduces(q):
+                part[k, half, :, :, wide] = acc[:, half]
+        pairs[k].start()
+
+    def combine(k):
+        pairs[k].wait_recv()
+        pair[k] = (part[k, c].astype(jnp.float32) + sib[k].astype(jnp.float32)).astype(jnp.bfloat16)
+        for copy in reduces(k):
             copy.start()
 
-    def collect(q):
-        for copy in reduces(q):
+    def collect(k):
+        for copy in reduces(k):
             copy.wait_recv()
-        total = pair[q, z].astype(jnp.float32)
+        total = pair[k, z].astype(jnp.float32)
         for i in range(CHIPS - 1):
-            total = total + got[q, i].astype(jnp.float32)
-        done[q] = total.astype(jnp.bfloat16)
-        pl.when(s != q)(deliver(q, s).start)
-
-        @pl.when(s == q)
+            total = total + got[k, i].astype(jnp.float32)
+        done[k] = total.astype(jnp.bfloat16)
+        pl.when(s != k // 2)(deliver(k, s).start)
+
+        @pl.when(s == k // 2)
         def _():
-            res[q] = done[q]
+            res[k // 2, k % 2] = done[k]
+
+    def advance(k):
+        project(k)
+        if k > 0:
+            combine(k - 1)
+        if k > 1:
+            collect(k - 2)
 
     state = jnp.zeros((STATE, WIDE), jnp.float32)
     local = to[:, :1]
@@ -593,39 +625,42 @@
         if q == 1:
             sums.relay(7)
         gate = sums.final(4 + q).astype(jnp.float32)
-        held[s, q] = (y * silu(gate)).astype(jnp.bfloat16)
-        for copy in gathers[q]:
-            copy.start()
+        gated = (y * silu(gate)).reshape(2 * CHIPS, 2, few_rows, WIDE)
+        for half in range(2):
+            held[s, 2 * q + half] = gated[:, half].reshape(SPAN // 2, WIDE).astype(jnp.bfloat16)
+            for copy in gathers[2 * q + half]:
+                copy.start()
         if q:
-            project(q - 1)
-        if q > 1:
-            combine(q - 2)
-    project(SEQS - 1)
-    combine(SEQS - 2)
-    collect(0)
-    collect(SEQS - 3)
-    combine(SEQS - 1)
-    collect(SEQS - 2)
-    collect(SEQS - 1)
+            advance(2 * q - 2)
+            advance(2 * q - 1)
+    last_k = 2 * SEQS - 1
+    advance(last_k - 1)
+    advance(last_k)
+    combine(last_k)
+    collect(last_k - 1)
+    collect(last_k)
     for q in range(SEQS):
-        pl.when(s != q)(deliver(0, q).wait_recv)
-        out_ref[:, q * cols_out : (q + 1) * cols_out] = res[q]
+        for half in range(2):
+            pl.when(s != q)(deliver(half, q).wait_recv)
+            out_ref[half * few_rows : (half + 1) * few_rows, q * cols_out : (q + 1) * cols_out] = res[q, half]
 
     for zb in range(CHIPS):
-        up, down, over, goes_up, goes_down = hops(zb)
-        pl.when(goes_up)(up.wait_send)
-        pl.when(goes_down)(down.wait_send)
-        over.wait_send()
-    for copy in spread + steps + [edge] + swaps + groups:
+        for r in range(SEQS):
+            up, down, over, goes_up, goes_down = hops(zb, r)
+            pl.when(goes_up)(up.wait_send)
+            pl.when(goes_down)(down.wait_send)
+            over.wait_send()
+    for copy in spread + steps + swaps + groups:
         copy.wait_send()
-    for q in range(SEQS):
-        for copy in gathers[q] + [pairs[q]] + reduces(q):
+    for k in range(2 * SEQS):
+        for copy in gathers[k] + [pairs[k]] + reduces(k):
             copy.wait_send()
-        pl.when(s != q)(deliver(q, s).wait_send)
+        pl.when(s != k // 2)(deliver(k, s).wait_send)
     for u in range(8):
         sums.drain(u)
     for u in range(4):
         sumb.drain(u)
+    sumh.drain(0)
 
 
 def mix(operands, own, seqs):
@@ -654,29 +689,30 @@
             pltpu.VMEM((16 + total, WIDE), f32),
             pltpu.VMEM((total, WIDE), f32),
             pltpu.VMEM((16 + SPAN, WIDE), f32),
-            pltpu.VMEM((2, 16, WIDE), bf),
+            pltpu.VMEM((SEQS, 16, WIDE), f32),
             pltpu.VMEM((GROUPS, 32, SPAN), bf),
             pltpu.VMEM((SEQS, GROUPS, 32, SPAN), bf),
             pltpu.VMEM((2, SEQS, OWN, WIDE), f32),
             pltpu.VMEM((16, total), bf),
             pltpu.VMEM((3, 16, total), bf),
             pltpu.VMEM((16, total), f32),
-            pltpu.VMEM((SEQS, SEQS, SPAN, WIDE), bf),
-            pltpu.VMEM((SPAN, SEQS * WIDE), bf),
-            pltpu.VMEM((SEQS, 2, CHIPS, OWN, cols), bf),
-            pltpu.VMEM((SEQS, CHIPS, OWN, cols), bf),
-            pltpu.VMEM((SEQS, CHIPS, OWN, cols), bf),
-            pltpu.VMEM((SEQS, CHIPS - 1, OWN, cols), bf),
-            pltpu.VMEM((SEQS, OWN, cols), bf),
-            pltpu.VMEM((SEQS, OWN, cols), bf),
+            pltpu.VMEM((SEQS, 2 * SEQS, SPAN // 2, WIDE), bf),
+            pltpu.VMEM((SPAN // 2, SEQS * WIDE), bf),
+            pltpu.VMEM((2 * SEQS, 2, CHIPS, OWN // 2, cols), bf),
+            pltpu.VMEM((2 * SEQS, CHIPS, OWN // 2, cols), bf),
+            pltpu.VMEM((2 * SEQS, CHIPS, OWN // 2, cols), bf),
+            pltpu.VMEM((2 * SEQS, CHIPS - 1, OWN // 2, cols), bf),
+            pltpu.VMEM((2 * SEQS, OWN // 2, cols), bf),
+            pltpu.VMEM((SEQS, 2, OWN // 2, cols), bf),
         ]
         + sums(8, SPAN)
         + sums(4, 2 * OWN)
+        + sums(1, 16)
         + [
-            dma((15,)), dma((3,)), dma((3,)), dma((4,)), dma((4,)), dma((4,)), dma((4,)), dma((4,)),
+            dma((15,)), dma((3,)), dma((3,)), dma((4, 4)), dma((4, 4)), dma((4, 4)), dma((4, 4)), dma((4, 4)),
             dma((8, 4)), dma((8, 4)), dma((4, 4)), dma((4, 4)),
-            dma, dma, dma((3,)), dma((3,)), dma((7,)), dma((7,)), dma((3,)), dma((3,)),
-            dma((4, 3)), dma((4, 3)), dma((4,)), dma((4,)), dma((4, 3)), dma((4, 3)), dma((4,)), dma((4,)),
+            dma((1, 4)), dma((1, 4)), dma((3,)), dma((3,)), dma((7,)), dma((7,)), dma((3,)), dma((3,)),
+            dma((8, 3)), dma((8, 3)), dma((8,)), dma((8,)), dma((8, 3)), dma((8, 3)), dma((8,)), dma((4, 2)),
         ],
         compiler_params=pltpu.CompilerParams(
             collective_id=2, has_side_effects=True, vmem_limit_bytes=56 * 2**20

time: 117 us -> 103 us (0.88)
  Pallas kernels: 115 us -> 101 us
    pallas_call x1, Pallas kernels: 115 us -> 101 us  [mix(): pl.pallas_call(mix_kernel, out_shape=jax.ShapeDtypeStruct((own, cols * se...]
where the time goes in v3:
time: 103 us
  Pallas kernels  101 us (98%)
  local copies, waits for them, and re-layouts  1.67 us (2%)
    pallas_call x1, Pallas kernels, mix(): pl.pallas_call(mix_kernel, out_shape=jax.ShapeDtypeStruct((own, cols * se...  101 us

profile of v3, /device:TPU:0, one launch (start us, length us, event | category | flops | bytes accessed | tf_op | source)
XLA Modules:
  0.0 103.1 jit_solution(11322260281037576501)
XLA Ops:
  0.0 101.4 %shard_map.145 = bf16[32,4096]{1,0:T(8,128)(2,1)} custom-call(bf16[32,4096]{1,0:T(8,128)(2,1)} %tok_hbm.1, bf16[1024,1024]{1,0:T(8,128)(2,1)} %wg_hbm.1, bf16[1024,1024]{1,0:T(8,128)(2,1)} %wx_hbm.1, bf16[1024,256]{1,0:T(8,128)(2,1)} %wb_hbm.1, bf16[16,1024]{1,0:T(8,128)(2,1)} %bitcast.4, f32[4,1024]{1,0:T(4,128)} %cx_hbm.1, f32[1,1024]{1,0:T(1,128)} %bitcast.5, ...), custom_call_target="tpu_custom_call" | custom-call | tf_op jit(solution)/shard_map/pallas_call | solution.py:679
  101.4 1.7 %copy.17 = bf16[32,4096]{1,0:T(8,128)(2,1)} copy(bf16[32,4096]{1,0:T(8,128)(2,1)} %shard_map.145) | data formatting | bytes 524288

commit v4 on v3

--- a/solution.py
+++ b/solution.py
@@ -287,16 +287,17 @@
     tok_hbm, wg_hbm, wx_hbm, wb_hbm, wdt_hbm, cx_hbm, cxb_hbm, cb_hbm, cbb_hbm, gain_hbm, wo_hbm,
     bias_hbm, rate_hbm, skip_hbm, len_hbm, out_ref,
     wg, wx, wb, wdt, cx, cxb, cb, cbb, gain, wo, bias_s, rate_s, skip_s, len_s,
-    tok, rel, xs, xc, bs, halo, bct, bca, bcp, dts, dtg, dtv,
+    tok, rel, xs, xc, gs, bs, halo, bct, bca, bcp, dtp, dts, dtg, dtv,
     held, normed, part, sib, pair, got, done, res,
     *rest,
 ):
     big, rest = rest[:11], rest[11:]
     few, rest = rest[:11], rest[11:]
     rim, rest = rest[:11], rest[11:]
+    three, rest = rest[:11], rest[11:]
     (
         w_sem, t_send, t_recv, zu_send, zd_send, z_recv, f_send, f_recv,
-        g_send, g_recv, b_send, b_recv, h_send, h_recv, d_send, d_recv,
+        g_send, g_recv, v_send, v_recv, b_send, b_recv, h_send, h_recv, d_send, d_recv,
         e_send, e_recv, a_send, a_recv,
         y_send, y_recv, p_send, p_recv, r_send, r_recv, o_send, o_recv,
     ) = rest
@@ -372,6 +373,7 @@
             pl.when(which)(lambda: arrive(i, pieces))
 
     sums = Sums(big, (g_send, g_recv), s, z, c)
+    sumg = Sums(three, (v_send, v_recv), s, z, c)
     sumb = Sums(few, (b_send, b_recv), s, z, c)
     sumh = Sums(rim, (h_send, h_recv), s, z, c)
 
@@ -410,6 +412,9 @@
         if i == 0:
             loads[3].wait()
         sums.emit(i, product(rows, wx))
+        if i == 0:
+            loads[5].wait()
+            sums.emit(CHIPS, product(rows, wg))
         if i:
             sumb.relay(i - 1)
             sums.relay(i - 1)
@@ -419,8 +424,12 @@
     def span_rows(q):
         return tok[:, :, q].reshape(SPAN, depth)
 
-    loads[5].wait()
-    sums.emit(4, product(span_rows(0), wg))
+    sums.relay(CHIPS)
+    def other_rows(q):
+        rows = [tok[zb, :, q].reshape(2 * OWN, depth) for zb in order[1:]]
+        return jnp.concatenate(rows, axis=0)
+
+    sumg.emit(0, product(other_rows(0), wg))
     bs[:16, :] = sumh.final(0).astype(jnp.float32)
     for i in range(CHIPS):
         bs[pl.ds(pl.multiple_of(16 + order[i] * 2 * OWN, 16), 2 * OWN), :] = sumb.final(i).astype(jnp.float32)
@@ -453,16 +462,20 @@
         copy.start()
     bca[s, t] = bct[t]
     sums.relay(CHIPS - 1)
+    heads = 4
     for q in range(SEQS):
-        dts[:, q * SPAN : (q + 1) * SPAN] = lax.dot_general(
+        some = lax.dot_general(
             wdt[...], span_rows(q), (((1,), (1,)), ((), ())), preferred_element_type=jnp.float32
-        ).astype(jnp.bfloat16)
+        )
+        for d in range(SEQS):
+            dtp[d, heads * q : heads * (q + 1), :] = some[heads * d : heads * (d + 1), :]
+    dts[...] = dtp[...].astype(jnp.bfloat16)
     steps = [
-        remote(dts, dtg.at[i], d_send.at[i], d_recv.at[i], peer) for i, peer in enumerate(along)
+        remote(dts.at[peer[0]], dtg.at[i], d_send.at[i], d_recv.at[i], peer) for i, peer in enumerate(along)
     ]
     for copy in steps:
         copy.start()
-    sums.emit(5, product(span_rows(1), wg))
+    sumg.emit(1, product(other_rows(1), wg))
     for copy in swaps:
         copy.wait_recv()
     groups = [
@@ -471,38 +484,41 @@
     ]
     for copy in groups:
         copy.start()
-    sums.relay(4)
+    sumg.relay(0)
     for i in range(CHIPS):
         full = sums.final(i).astype(jnp.float32).reshape(2, SEQS, OWN, WIDE)
         for half in range(2):
             for q in range(SEQS):
                 at = 16 + q * SPAN + half * OWN + order[i] * 2 * OWN
                 xs[pl.ds(pl.multiple_of(at, 16), OWN), :] = full[half, q]
-    sums.emit(6, product(span_rows(2), wg))
+    sumg.emit(2, product(other_rows(2), wg))
+    full = sums.final(CHIPS).astype(jnp.float32).reshape(2, SEQS, OWN, WIDE)
+    for half in range(2):
+        for q in range(SEQS):
+            gs[q, pl.ds(pl.multiple_of(z * 2 * OWN + half * OWN, 16), OWN), :] = full[half, q]
     xs[:16, :] = jnp.zeros((16, WIDE), jnp.float32)
     mine = pl.ds(pl.multiple_of(s * WIDE, WIDE), WIDE)
     for q in range(SEQS):
         xc[q * SPAN : (q + 1) * SPAN, :] = conv(
             xs, 16 + q * SPAN, cx[:, mine], cxb[:, mine], rel[q * SPAN : (q + 1) * SPAN, :1]
         ).astype(jnp.float32)
-    sums.relay(5)
-    sums.emit(7, product(span_rows(3), wg))
+    sumg.relay(1)
+    sumg.emit(3, product(other_rows(3), wg))
     for copy in steps:
         copy.wait_recv()
-    dtv[...] = (
-        dts[...].astype(jnp.float32)
-        + dtg[0].astype(jnp.float32)
-        + dtg[1].astype(jnp.float32)
-        + dtg[2].astype(jnp.float32)
-    ).astype(jnp.bfloat16).astype(jnp.float32)
-    heads = 4
-    line = lax.broadcasted_iota(jnp.int32, (8, total), 0)
-    dt8, rate8 = jnp.zeros((8, total), jnp.float32), jnp.zeros((8, total), jnp.float32)
+    small = dts[s].astype(jnp.float32)
+    for i in range(SEQS - 1):
+        small = small + dtg[i].astype(jnp.float32)
+    line = to[: heads * SEQS, :] % heads
+    bias, rate = jnp.zeros(line.shape, jnp.float32), jnp.zeros(line.shape, jnp.float32)
     for h in range(heads):
-        row = dtv[pl.ds(heads * s + h, 1), :] + bias_s[heads * s + h]
-        row = jnp.maximum(row, 0.0) + jnp.log1p(jnp.exp(-jnp.abs(row)))
-        dt8 = jnp.where(line == h, row, dt8)
-        dt8 = jnp.where(line == heads + h, row * (-LOG2E * rate_s[heads * s + h]), dt8)
+        bias = jnp.where(line == h, bias_s[heads * s + h], bias)
+        rate = jnp.where(line == h, -LOG2E * rate_s[heads * s + h], rate)
+    small = small.astype(jnp.bfloat16).astype(jnp.float32) + bias
+    small = jnp.maximum(small, 0.0) + jnp.log1p(jnp.exp(-jnp.abs(small)))
+    for q in range(SEQS):
+        dtv[q, :heads, :] = small[heads * q : heads * (q + 1), :]
+        dtv[q, heads:, :] = (small * rate)[heads * q : heads * (q + 1), :]
 
     dif = to - frm
     upto = (dif <= 0).astype(jnp.float32)
@@ -540,14 +556,15 @@
     def project(k):
         for copy in gathers[k]:
             copy.wait_recv()
-        squares = jnp.zeros((SPAN // 2, WIDE), jnp.float32)
-        for n in range(SEQS):
-            piece = held[n, k].astype(jnp.float32)
+        squares = jnp.zeros((SPAN // 2, HALF), jnp.float32)
+        for n in range(2 * SEQS):
+            piece = held[n // 2, k, n % 2].astype(jnp.float32)
             squares = squares + piece * piece
         scale = lax.rsqrt(jnp.sum(squares, axis=1, keepdims=True) / (SEQS * WIDE) + 1e-05)
-        for n in range(SEQS):
-            wide = slice(n * WIDE, (n + 1) * WIDE)
-            normed[:, wide] = (held[n, k].astype(jnp.float32) * scale * gain[:, wide]).astype(jnp.bfloat16)
+        for n in range(2 * SEQS):
+            wide = slice(n * HALF, (n + 1) * HALF)
+            piece = held[n // 2, k, n % 2].astype(jnp.float32)
+            normed[:, wide] = (piece * scale * gain[:, wide]).astype(jnp.bfloat16)
         for n in range(cols_out // WIDE):
             wide = slice(n * WIDE, (n + 1) * WIDE)
             acc = jnp.dot(normed[...], wo[:, wide], preferred_element_type=jnp.float32)
@@ -591,9 +608,9 @@
         cn = bca[q, 4:].reshape(STATE, SPAN).astype(jnp.float32).T.astype(jnp.bfloat16)
         scores = jnp.dot(cn, bt, preferred_element_type=jnp.float32)
         scores = jnp.where((dif >= 0) & (dif <= away), scores, 0.0)
-        both = dt8[:, here]
+        both = dtv[q]
         cum = jnp.dot(both, upto, precision=HIGH, preferred_element_type=jnp.float32)
-        both = jnp.where(line[:, :SPAN] < heads, both, cum)
+        both = jnp.where(to[:8, :] < heads, both, cum)
         cols = jnp.concatenate([both, jnp.zeros((HALF - 8, SPAN), jnp.float32)], axis=0).T
 
         def expand(first):
@@ -621,21 +638,27 @@
         state = carry[SPAN - 1 :, :] * state + fresh
         y = inner + outer * carry + skip * xv
         if q == 0:
-            sums.relay(6)
+            sumg.relay(2)
         if q == 1:
-            sums.relay(7)
-        gate = sums.final(4 + q).astype(jnp.float32)
+            sumg.relay(3)
+        some = sumg.final(q).astype(jnp.float32)
+        for i in range(1, CHIPS):
+            to_rows = pl.ds(pl.multiple_of(order[i] * 2 * OWN, 16), 2 * OWN)
+            gs[q, to_rows, :] = some[(i - 1) * 2 * OWN : i * 2 * OWN]
+        gate = gs[q]
         gated = (y * silu(gate)).reshape(2 * CHIPS, 2, few_rows, WIDE)
         for half in range(2):
-            held[s, 2 * q + half] = gated[:, half].reshape(SPAN // 2, WIDE).astype(jnp.bfloat16)
-            for copy in gathers[2 * q + half]:
+            k = 2 * q + half
+            some = gated[:, half].reshape(SPAN // 2, WIDE).astype(jnp.bfloat16)
+            held[s, k, 0], held[s, k, 1] = some[:, :HALF], some[:, HALF:]
+            for copy in gathers[k]:
                 copy.start()
-        if q:
-            advance(2 * q - 2)
-            advance(2 * q - 1)
+        for k in range(2 * q - 4, 2 * q - 2):
+            if k >= 0:
+                advance(k)
     last_k = 2 * SEQS - 1
-    advance(last_k - 1)
-    advance(last_k)
+    for k in range(last_k - 3, last_k + 1):
+        advance(k)
     combine(last_k)
     collect(last_k - 1)
     collect(last_k)
@@ -656,8 +679,10 @@
         for copy in gathers[k] + [pairs[k]] + reduces(k):
             copy.wait_send()
         pl.when(s != k // 2)(deliver(k, s).wait_send)
-    for u in range(8):
+    for u in range(5):
         sums.drain(u)
+    for u in range(4):
+        sumg.drain(u)
     for u in range(4):
         sumb.drain(u)
     sumh.drain(0)
@@ -688,15 +713,17 @@
             pltpu.VMEM((total, HALF), jnp.int32),
             pltpu.VMEM((16 + total, WIDE), f32),
             pltpu.VMEM((total, WIDE), f32),
+            pltpu.VMEM((SEQS, SPAN, WIDE), f32),
             pltpu.VMEM((16 + SPAN, WIDE), f32),
             pltpu.VMEM((SEQS, 16, WIDE), f32),
             pltpu.VMEM((GROUPS, 32, SPAN), bf),
             pltpu.VMEM((SEQS, GROUPS, 32, SPAN), bf),
             pltpu.VMEM((2, SEQS, OWN, WIDE), f32),
-            pltpu.VMEM((16, total), bf),
-            pltpu.VMEM((3, 16, total), bf),
-            pltpu.VMEM((16, total), f32),
-            pltpu.VMEM((SEQS, 2 * SEQS, SPAN // 2, WIDE), bf),
+            pltpu.VMEM((SEQS, 16, SPAN), f32),
+            pltpu.VMEM((SEQS, 16, SPAN), bf),
+            pltpu.VMEM((3, 16, SPAN), bf),
+            pltpu.VMEM((SEQS, 8, SPAN), f32),
+            pltpu.VMEM((SEQS, 2 * SEQS, 2, SPAN // 2, HALF), bf),
             pltpu.VMEM((SPAN // 2, SEQS * WIDE), bf),
             pltpu.VMEM((2 * SEQS, 2, CHIPS, OWN // 2, cols), bf),
             pltpu.VMEM((2 * SEQS, CHIPS, OWN // 2, cols), bf),
@@ -705,12 +732,13 @@
             pltpu.VMEM((2 * SEQS, OWN // 2, cols), bf),
             pltpu.VMEM((SEQS, 2, OWN // 2, cols), bf),
         ]
-        + sums(8, SPAN)
-        + sums(4, 2 * OWN)
+        + sums(CHIPS + 1, SPAN)
+        + sums(CHIPS, 2 * OWN)
         + sums(1, 16)
+        + sums(SEQS, SPAN - 2 * OWN)
         + [
             dma((15,)), dma((3,)), dma((3,)), dma((4, 4)), dma((4, 4)), dma((4, 4)), dma((4, 4)), dma((4, 4)),
-            dma((8, 4)), dma((8, 4)), dma((4, 4)), dma((4, 4)),
+            dma((5, 4)), dma((5, 4)), dma((4, 4)), dma((4, 4)), dma((4, 4)), dma((4, 4)),
             dma((1, 4)), dma((1, 4)), dma((3,)), dma((3,)), dma((7,)), dma((7,)), dma((3,)), dma((3,)),
             dma((8, 3)), dma((8, 3)), dma((8,)), dma((8,)), dma((8, 3)), dma((8, 3)), dma((8,)), dma((4, 2)),
         ],

time: 103 us -> 97.6 us (0.948)
  Pallas kernels: 101 us -> 95.7 us
    pallas_call x1, Pallas kernels: 101 us -> 95.7 us  [mix(): pl.pallas_call(mix_kernel, out_shape=jax.ShapeDtypeStruct((own, cols * se...]
where the time goes in v4:
time: 97.6 us; the launch traced here: 97.4 us
  Pallas kernels  95.7 us (98%)
  local copies, waits for them, and re-layouts  1.67 us (2%)
    pallas_call x1, Pallas kernels, mix(): pl.pallas_call(mix_kernel, out_shape=jax.ShapeDtypeStruct((own, cols * se...  95.7 us

profile of v4, /device:TPU:0, one launch (start us, length us, event | category | flops | bytes accessed | tf_op | source)
XLA Modules:
  0.0 97.4 jit_solution(16137694759708142753)
XLA Ops:
  0.0 95.7 %shard_map.145 = bf16[32,4096]{1,0:T(8,128)(2,1)} custom-call(bf16[32,4096]{1,0:T(8,128)(2,1)} %tok_hbm.1, bf16[1024,1024]{1,0:T(8,128)(2,1)} %wg_hbm.1, bf16[1024,1024]{1,0:T(8,128)(2,1)} %wx_hbm.1, bf16[1024,256]{1,0:T(8,128)(2,1)} %wb_hbm.1, bf16[16,1024]{1,0:T(8,128)(2,1)} %bitcast.4, f32[4,1024]{1,0:T(4,128)} %cx_hbm.1, f32[1,1024]{1,0:T(1,128)} %bitcast.5, ...), custom_call_target="tpu_custom_call" | custom-call | tf_op jit(solution)/shard_map/pallas_call | solution.py:704
  95.8 1.7 %copy.17 = bf16[32,4096]{1,0:T(8,128)(2,1)} copy(bf16[32,4096]{1,0:T(8,128)(2,1)} %shard_map.145) | data formatting | bytes 524288

commit v5 on v4

--- a/solution.py
+++ b/solution.py
@@ -288,7 +288,7 @@
     bias_hbm, rate_hbm, skip_hbm, len_hbm, out_ref,
     wg, wx, wb, wdt, cx, cxb, cb, cbb, gain, wo, bias_s, rate_s, skip_s, len_s,
     tok, rel, xs, xc, gs, bs, halo, bct, bca, bcp, dtp, dts, dtg, dtv,
-    held, normed, part, sib, pair, got, done, res,
+    held, normed, part, sib, pair, got, done,
     *rest,
 ):
     big, rest = rest[:11], rest[11:]
@@ -526,8 +526,6 @@
     skip = jnp.zeros((1, WIDE), jnp.float32)
     for h in range(heads):
         skip = jnp.where(lane[:1] == h, skip_s[heads * s + h], skip)
-    for copy in groups:
-        copy.wait_recv()
 
     cols_out = wo.shape[1]
     few_rows = OWN // 2
@@ -550,8 +548,15 @@
             for i, to in enumerate(peers)
         ]
 
+    def place(frm, half):
+        cols = pl.ds(pl.multiple_of(frm * cols_out, cols_out), cols_out)
+        return out_ref.at[half * few_rows : (half + 1) * few_rows, cols]
+
     def deliver(k, frm):
-        return remote(done.at[k], res.at[frm, k % 2], o_send.at[k], o_recv.at[frm, k % 2], (k // 2, t))
+        return remote(done.at[k], place(frm, k % 2), o_send.at[k], o_recv.at[frm, k % 2], (k // 2, t))
+
+    def keep(k):
+        return pltpu.make_async_copy(done.at[k], place(s, k % 2), o_send.at[k])
 
     def project(k):
         for copy in gathers[k]:
@@ -587,15 +592,11 @@
             total = total + got[k, i].astype(jnp.float32)
         done[k] = total.astype(jnp.bfloat16)
         pl.when(s != k // 2)(deliver(k, s).start)
-
-        @pl.when(s == k // 2)
-        def _():
-            res[k // 2, k % 2] = done[k]
+        pl.when(s == k // 2)(keep(k).start)
 
     def advance(k):
         project(k)
-        if k > 0:
-            combine(k - 1)
+        combine(k)
         if k > 1:
             collect(k - 2)
 
@@ -604,6 +605,8 @@
     for q in range(SEQS):
         here = slice(q * SPAN, (q + 1) * SPAN)
         away = rel[here, :1]
+        for i, copy in enumerate(groups):
+            pl.when((s ^ (i + 1)) == q)(copy.wait_recv)
         bt = bca[q, :4].reshape(STATE, SPAN)
         cn = bca[q, 4:].reshape(STATE, SPAN).astype(jnp.float32).T.astype(jnp.bfloat16)
         scores = jnp.dot(cn, bt, preferred_element_type=jnp.float32)
@@ -659,13 +662,11 @@
     last_k = 2 * SEQS - 1
     for k in range(last_k - 3, last_k + 1):
         advance(k)
-    combine(last_k)
     collect(last_k - 1)
     collect(last_k)
     for q in range(SEQS):
         for half in range(2):
             pl.when(s != q)(deliver(half, q).wait_recv)
-            out_ref[half * few_rows : (half + 1) * few_rows, q * cols_out : (q + 1) * cols_out] = res[q, half]
 
     for zb in range(CHIPS):
         for r in range(SEQS):
@@ -679,6 +680,7 @@
         for copy in gathers[k] + [pairs[k]] + reduces(k):
             copy.wait_send()
         pl.when(s != k // 2)(deliver(k, s).wait_send)
+        pl.when(s == k // 2)(keep(k).wait)
     for u in range(5):
         sums.drain(u)
     for u in range(4):
@@ -705,7 +707,7 @@
         mix_kernel,
         out_shape=jax.ShapeDtypeStruct((own, cols * seqs), bf),
         in_specs=[pl.BlockSpec(memory_space=pl.ANY)] * len(operands),
-        out_specs=pl.BlockSpec(memory_space=pltpu.VMEM),
+        out_specs=pl.BlockSpec(memory_space=pl.ANY),
         scratch_shapes=[pltpu.VMEM(a.shape, a.dtype) for a in operands[1:11]]
         + [pltpu.SMEM(a.shape, a.dtype) for a in operands[11:]]
         + [
@@ -730,7 +732,6 @@
             pltpu.VMEM((2 * SEQS, CHIPS, OWN // 2, cols), bf),
             pltpu.VMEM((2 * SEQS, CHIPS - 1, OWN // 2, cols), bf),
             pltpu.VMEM((2 * SEQS, OWN // 2, cols), bf),
-            pltpu.VMEM((SEQS, 2, OWN // 2, cols), bf),
         ]
         + sums(CHIPS + 1, SPAN)
         + sums(CHIPS, 2 * OWN)

time: 97.6 us -> 95.2 us (0.975)
  Pallas kernels: 95.7 us -> 93.3 us
    pallas_call x1, Pallas kernels: 95.7 us -> 93.3 us  [mix(): pl.pallas_call(mix_kernel, out_shape=jax.ShapeDtypeStruct((own, cols * se...]
where the time goes in v5:
time: 95.2 us; the launch traced here: 95 us
  Pallas kernels  93.3 us (98%)
  local copies, waits for them, and re-layouts  1.67 us (2%)
    pallas_call x1, Pallas kernels, mix(): pl.pallas_call(mix_kernel, out_shape=jax.ShapeDtypeStruct((own, cols * se...  93.3 us

profile of v5, /device:TPU:0, one launch (start us, length us, event | category | flops | bytes accessed | tf_op | source)
XLA Modules:
  0.0 95.0 jit_solution(11447205622608557070)
XLA Ops:
  0.0 93.3 %shard_map.145 = bf16[32,4096]{1,0:T(8,128)(2,1)} custom-call(bf16[32,4096]{1,0:T(8,128)(2,1)} %tok_hbm.1, bf16[1024,1024]{1,0:T(8,128)(2,1)} %wg_hbm.1, bf16[1024,1024]{1,0:T(8,128)(2,1)} %wx_hbm.1, bf16[1024,256]{1,0:T(8,128)(2,1)} %wb_hbm.1, bf16[16,1024]{1,0:T(8,128)(2,1)} %bitcast.4, f32[4,1024]{1,0:T(4,128)} %cx_hbm.1, f32[1,1024]{1,0:T(1,128)} %bitcast.5, ...), custom_call_target="tpu_custom_call" | custom-call | tf_op jit(solution)/shard_map/pallas_call | solution.py:706
  93.3 1.7 %copy.17 = bf16[32,4096]{1,0:T(8,128)(2,1)} copy(bf16[32,4096]{1,0:T(8,128)(2,1)} %shard_map.145) | data formatting | bytes 524288

commit v6 on v5

--- a/solution.py
+++ b/solution.py
@@ -328,7 +328,7 @@
         )
         for i, peer in enumerate(along)
     ]
-    for copy in spread:
+    for copy in spread[::-1]:
         copy.start()
     loads[0].wait()
 
@@ -594,6 +594,13 @@
         pl.when(s != k // 2)(deliver(k, s).start)
         pl.when(s == k // 2)(keep(k).start)
 
+    def settle(first, end):
+        for k in range(first, end):
+            for copy in gathers[k] + [pairs[k]] + reduces(k):
+                copy.wait_send()
+            pl.when(s != k // 2)(deliver(k, s).wait_send)
+            pl.when(s == k // 2)(keep(k).wait)
+
     def advance(k):
         project(k)
         combine(k)
@@ -642,8 +649,6 @@
         y = inner + outer * carry + skip * xv
         if q == 0:
             sumg.relay(2)
-        if q == 1:
-            sumg.relay(3)
         some = sumg.final(q).astype(jnp.float32)
         for i in range(1, CHIPS):
             to_rows = pl.ds(pl.multiple_of(order[i] * 2 * OWN, 16), 2 * OWN)
@@ -656,18 +661,12 @@
             held[s, k, 0], held[s, k, 1] = some[:, :HALF], some[:, HALF:]
             for copy in gathers[k]:
                 copy.start()
+        if q == 0:
+            sumg.relay(3)
         for k in range(2 * q - 4, 2 * q - 2):
             if k >= 0:
                 advance(k)
     last_k = 2 * SEQS - 1
-    for k in range(last_k - 3, last_k + 1):
-        advance(k)
-    collect(last_k - 1)
-    collect(last_k)
-    for q in range(SEQS):
-        for half in range(2):
-            pl.when(s != q)(deliver(half, q).wait_recv)
-
     for zb in range(CHIPS):
         for r in range(SEQS):
             up, down, over, goes_up, goes_down = hops(zb, r)
@@ -676,11 +675,6 @@
             over.wait_send()
     for copy in spread + steps + swaps + groups:
         copy.wait_send()
-    for k in range(2 * SEQS):
-        for copy in gathers[k] + [pairs[k]] + reduces(k):
-            copy.wait_send()
-        pl.when(s != k // 2)(deliver(k, s).wait_send)
-        pl.when(s == k // 2)(keep(k).wait)
     for u in range(5):
         sums.drain(u)
     for u in range(4):
@@ -688,6 +682,16 @@
     for u in range(4):
         sumb.drain(u)
     sumh.drain(0)
+    for k in range(last_k - 3, last_k + 1):
+        advance(k)
+    settle(0, last_k - 2)
+    collect(last_k - 1)
+    collect(last_k)
+    for q in range(SEQS):
+        for half in range(2):
+            pl.when(s != q)(deliver(half, q).wait_recv)
+
+    settle(last_k - 2, last_k + 1)
 
 
 def mix(operands, own, seqs):

time: 95.2 us -> 94.7 us (level)
  Pallas kernels: 93.3 us -> 92.3 us
    pallas_call x1, Pallas kernels: 93.3 us -> 92.3 us  [mix(): pl.pallas_call(mix_kernel, out_shape=jax.ShapeDtypeStruct((own, cols * se...]
where the time goes in v6:
time: 94.7 us; the launch traced here: 93.9 us
  Pallas kernels  92.3 us (97%)
  local copies, waits for them, and re-layouts  1.67 us (2%)
    pallas_call x1, Pallas kernels, mix(): pl.pallas_call(mix_kernel, out_shape=jax.ShapeDtypeStruct((own, cols * se...  92.3 us

profile of v6, /device:TPU:0, one launch (start us, length us, event | category | flops | bytes accessed | tf_op | source)
XLA Modules:
  0.0 93.9 jit_solution(11134077124511390281)
XLA Ops:
  0.0 92.3 %shard_map.145 = bf16[32,4096]{1,0:T(8,128)(2,1)} custom-call(bf16[32,4096]{1,0:T(8,128)(2,1)} %tok_hbm.1, bf16[1024,1024]{1,0:T(8,128)(2,1)} %wg_hbm.1, bf16[1024,1024]{1,0:T(8,128)(2,1)} %wx_hbm.1, bf16[1024,256]{1,0:T(8,128)(2,1)} %wb_hbm.1, bf16[16,1024]{1,0:T(8,128)(2,1)} %bitcast.4, f32[4,1024]{1,0:T(4,128)} %cx_hbm.1, f32[1,1024]{1,0:T(1,128)} %bitcast.5, ...), custom_call_target="tpu_custom_call" | custom-call | tf_op jit(solution)/shard_map/pallas_call | solution.py:710
  92.3 1.7 %copy.17 = bf16[32,4096]{1,0:T(8,128)(2,1)} copy(bf16[32,4096]{1,0:T(8,128)(2,1)} %shard_map.145) | data formatting | bytes 524288

commit v7 on v6

--- a/solution.py
+++ b/solution.py
@@ -430,6 +430,8 @@
         return jnp.concatenate(rows, axis=0)
 
     sumg.emit(0, product(other_rows(0), wg))
+    sumg.emit(1, product(other_rows(1), wg))
+    sums.relay(CHIPS - 1)
     bs[:16, :] = sumh.final(0).astype(jnp.float32)
     for i in range(CHIPS):
         bs[pl.ds(pl.multiple_of(16 + order[i] * 2 * OWN, 16), 2 * OWN), :] = sumb.final(i).astype(jnp.float32)
@@ -461,7 +463,6 @@
     for copy in swaps:
         copy.start()
     bca[s, t] = bct[t]
-    sums.relay(CHIPS - 1)
     heads = 4
     for q in range(SEQS):
         some = lax.dot_general(
@@ -475,7 +476,6 @@
     ]
     for copy in steps:
         copy.start()
-    sumg.emit(1, product(other_rows(1), wg))
     for copy in swaps:
         copy.wait_recv()
     groups = [

time: 94.7 us -> 94.7 us (level)
  no operation moved by 1% of the time
where the time goes in v7:
time: 94.7 us; the launch traced here: 93.9 us
  Pallas kernels  92.3 us (97%)
  local copies, waits for them, and re-layouts  1.67 us (2%)
    pallas_call x1, Pallas kernels, mix(): pl.pallas_call(mix_kernel, out_shape=jax.ShapeDtypeStruct((own, cols * se...  92.3 us

profile of v7, /device:TPU:0, one launch (start us, length us, event | category | flops | bytes accessed | tf_op | source)
XLA Modules:
  0.0 93.9 jit_solution(3711213398217926040)
XLA Ops:
  0.0 92.3 %shard_map.145 = bf16[32,4096]{1,0:T(8,128)(2,1)} custom-call(bf16[32,4096]{1,0:T(8,128)(2,1)} %tok_hbm.1, bf16[1024,1024]{1,0:T(8,128)(2,1)} %wg_hbm.1, bf16[1024,1024]{1,0:T(8,128)(2,1)} %wx_hbm.1, bf16[1024,256]{1,0:T(8,128)(2,1)} %wb_hbm.1, bf16[16,1024]{1,0:T(8,128)(2,1)} %bitcast.4, f32[4,1024]{1,0:T(4,128)} %cx_hbm.1, f32[1,1024]{1,0:T(1,128)} %bitcast.5, ...), custom_call_target="tpu_custom_call" | custom-call | tf_op jit(solution)/shard_map/pallas_call | solution.py:710
  92.3 1.7 %copy.17 = bf16[32,4096]{1,0:T(8,128)(2,1)} copy(bf16[32,4096]{1,0:T(8,128)(2,1)} %shard_map.145) | data formatting | bytes 524288
